TPU v7x, 32 devices: a whole 2x2x4 slice. The times are simulated.
32 devices in a mesh: grp: 8 (over z, x), seq: 4 (over y, core).
Axes of the slice: x: 2, y: 2, z: 4, core: 2. Of those that a mesh axis runs over, the one named last changes fastest.
Arguments:
- tokens: bfloat16 [4096, 768], P(('grp', 'seq')), may hold values from -6 to 6
- global_tokens: bfloat16 [512, 768], P('grp'), may hold values from -6 to 6
- neighbours: int32 [4096, 8], P(('grp', 'seq')), may hold values from 0 to 383
- token_ranks: int32 [2, 4096], P(None, ('grp', 'seq')), may hold values from 0 to 511
- membership: int32 [4096], P(('grp', 'seq')), may hold values from 0 to 63
- w_graph: bfloat16 [768, 768], replicated, may hold values from -0.625 to 0.625
- gain_one: float32 [768], replicated, may hold values from 0.5 to 1.5
- shift_one: float32 [768], replicated, may hold values from -1.75 to 1.75
- w_query: bfloat16 [768, 768], replicated, may hold values from -0.21875 to 0.21875
- w_key: bfloat16 [768, 768], replicated, may hold values from -0.21875 to 0.21875
- w_value: bfloat16 [768, 768], replicated, may hold values from -0.21875 to 0.21875
- rich_query: bfloat16 [64, 48], replicated, may hold values from -0.75 to 0.75
- rich_key: bfloat16 [64, 48], replicated, may hold values from -0.75 to 0.75
- w_out: bfloat16 [768, 768], replicated, may hold values from -1.25 to 1.25
- gain_two: float32 [768], replicated, may hold values from 0.5 to 1.5
- shift_two: float32 [768], replicated, may hold values from -1.75 to 1.75
- w_up: bfloat16 [768, 3072], replicated, may hold values from -0.21875 to 0.21875
- bias_up: float32 [3072], replicated, may hold values from -1.75 to 1.75
- w_down: bfloat16 [3072, 768], replicated, may hold values from -0.109375 to 0.109375
- bias_down: float32 [768], replicated, may hold values from -1.75 to 1.75
- cot_tokens: bfloat16 [4096, 768], P(('grp', 'seq')), may hold values from -6 to 6
- cot_global: bfloat16 [512, 768], P('grp'), may hold values from -6 to 6
Outputs:
- out_tokens: bfloat16 [4096, 768], P(('grp', 'seq'))
- out_global: bfloat16 [512, 768], P('grp')
- grad_tokens: float32 [4096, 768], P(('grp', 'seq'))
- grad_global: float32 [512, 768], P('grp')
- grad_w_graph: float32 [768, 768], P('seq')
- grad_gain_one: float32 [768], P('seq')
- grad_shift_one: float32 [768], P('seq')
- grad_w_query: float32 [768, 768], P('seq')
- grad_w_key: float32 [768, 768], P('seq')
- grad_w_value: float32 [768, 768], P('seq')
- grad_rich_query: float32 [64, 48], P('seq')
- grad_rich_key: float32 [64, 48], P('seq')
- grad_w_out: float32 [768, 768], P('seq')
- grad_gain_two: float32 [768], P('seq')
- grad_shift_two: float32 [768], P('seq')
- grad_w_up: float32 [768, 3072], P('seq')
- grad_bias_up: float32 [3072], P('seq')
- grad_w_down: float32 [3072, 768], P('seq')
- grad_bias_down: float32 [768], P('seq')
Inputs may be any that keep to these rules, and one draw needn't show every extreme that they name: neighbours[i, k] = n names position (i // 128) * 128 - 128 + n of i's sequence.
All inputs are finite; a program needn't handle non-finite values.
Results may differ from a plain program's by a relative error of at most 0.019.
Values may be sent and summed in bfloat16 or wider, within the bound.
No kernel may reach another device: no remote copies, remote signals or barrier semaphores. Data moves between devices by JAX's collectives and lax.ppermute only.
A program may use at most 192 MiB of HBM per device.

v0:
```python
import math

import jax
import jax.numpy as jnp
from jax import lax
from jax.sharding import PartitionSpec as P

D = 768
HEADS = 12
HEAD_DIM = 64
RADIUS = 128
GLOBALS = 64
NEIGH = 8
SEQ_TOKENS = 2048


EPSILON = 1e-05
PRECISE = lax.Precision.HIGHEST
MASKED = -1e30


def with_halo(cells, sides, width):
    for axis, dim in sides:
        count = lax.axis_size(axis)
        ends = count - 1
        head = lax.slice_in_dim(cells, 0, width, axis=dim)
        tail = lax.slice_in_dim(cells, cells.shape[dim] - width, cells.shape[dim], axis=dim)
        cells = jnp.concatenate(
            [
                lax.ppermute(tail, axis, [(i, (i + 1) % count) for i in range(ends)]),
                cells,
                lax.ppermute(head, axis, [((i + 1) % count, i) for i in range(ends)]),
            ],
            axis=dim,
        )
    return cells


def joined(array, axis, combine):
    everything = jax.tree.map(
        lambda part, kind: lax.all_gather(part.astype(kind), axis),
        array,
        (jnp.bfloat16, jnp.bfloat16, jnp.bfloat16),
    )

    def take(k):
        return jax.tree.map(lambda part, own: part[k].astype(own.dtype), everything, array)

    return lax.fori_loop(
        1, lax.axis_size(axis), lambda k, so_far: combine(so_far, take(k)), take(0)
    )


def shifted(block, axis, distance):
    devices = range(lax.axis_size(axis))
    route = [(i - distance, i) for i in devices if i - distance in devices]
    return lax.ppermute(block, axis, route)


def layer_norm(rows_in, gain_in, shift_in):
    row_mean = jnp.mean(rows_in, axis=-1, keepdims=True)
    centred = rows_in - row_mean
    variance = jnp.mean(centred * centred, axis=-1, keepdims=True)
    return centred * lax.rsqrt(variance + EPSILON) * gain_in + shift_in


def rich_part(a_block, b_window, rank_query, rank_key, log_norm):
    combined = None
    for coordinate in range(2):
        order_flag = (rank_query[coordinate][:, None] < rank_key[coordinate][None, :]).astype(
            jnp.float32
        )
        distance = (
            jnp.log1p(
                jnp.abs(rank_query[coordinate][:, None] - rank_key[coordinate][None, :]).astype(
                    jnp.float32
                )
            )
            / log_norm
        )
        order_logit = a_block[:, :, None, coordinate] + b_window[:, None, :, coordinate]
        centre = a_block[:, :, None, 2 + coordinate] + b_window[:, None, :, 2 + coordinate]
        pair_term = (
            order_flag * jax.nn.log_sigmoid(order_logit)
            + (1.0 - order_flag) * jax.nn.log_sigmoid(-order_logit)
            - 0.5 * (distance - centre) ** 2
        )
        combined = pair_term if combined is None else combined + pair_term
    return combined


def product(left, right):
    return jnp.dot(left, right, preferred_element_type=jnp.float32)


def product_left(left, right):
    return jnp.einsum("ta,tb->ab", left, right, preferred_element_type=jnp.float32)


def product_right(left, right):
    return jnp.einsum("tb,ab->ta", left, right, preferred_element_type=jnp.float32)


def local(
    tokens,
    global_tokens,
    neighbours,
    token_ranks,
    membership,
    w_graph,
    gain_one,
    shift_one,
    w_query,
    w_key,
    w_value,
    rich_query,
    rich_key,
    w_out,
    gain_two,
    shift_two,
    w_up,
    bias_up,
    w_down,
    bias_down,
    cot_tokens,
    cot_global,
):
    tok_count = tokens.shape[0]
    seq_count = lax.axis_size("seq")
    seq_index = lax.axis_index("seq")
    seq_len = min(SEQ_TOKENS, tok_count * seq_count)
    span = seq_len // tok_count
    group_seqs = global_tokens.shape[0] // GLOBALS
    seq_slot = seq_index // span
    seq_local = seq_index % span
    slot_flag = (jnp.arange(group_seqs, dtype=jnp.int32) == seq_slot).astype(jnp.float32)
    log_norm = math.log(1.0 + seq_len)
    score_scale = 1.0 / math.sqrt(HEAD_DIM)
    block_rows = min(512, tok_count)
    window = block_rows + 2 * RADIUS
    ext_count = tok_count + 2 * RADIUS
    first_flag = (seq_index == 0).astype(jnp.float32)
    own_pos = seq_local * tok_count + jnp.arange(tok_count, dtype=jnp.int32)
    ext_pos = seq_local * tok_count - RADIUS + jnp.arange(ext_count, dtype=jnp.int32)
    key_valid = (ext_pos >= 0) & (ext_pos < seq_len)

    def own_slot(array_in):
        return lax.dynamic_index_in_dim(array_in, seq_slot, 0, keepdims=False)

    def to_slots(array_in):
        return slot_flag.reshape((group_seqs,) + (1,) * array_in.ndim) * array_in[None]

    token_ext = with_halo(tokens, (("seq", 0),), RADIUS)
    token_ext = jnp.where(key_valid[:, None], token_ext, jnp.zeros_like(token_ext))
    flat_index = neighbours.reshape(-1)
    gathered = (
        jnp.take(token_ext, flat_index, axis=0).astype(jnp.float32).reshape(tok_count, NEIGH, D)
    )
    agg_low = jnp.mean(gathered, axis=1).astype(jnp.bfloat16)
    graph_pre = product(agg_low, w_graph)
    graph_out, graph_back = jax.vjp(jax.nn.gelu, graph_pre)
    super_rows = tokens.astype(jnp.float32) + graph_out
    normed_full, norm_back = jax.vjp(layer_norm, super_rows, gain_one, shift_one)
    normed = normed_full.astype(jnp.bfloat16)
    glob_in = global_tokens.astype(jnp.float32)
    glob_normed_full, glob_norm_back = jax.vjp(layer_norm, glob_in, gain_one, shift_one)
    glob_normed = glob_normed_full.astype(jnp.bfloat16)
    query = product(normed, w_query).astype(jnp.bfloat16)
    key_own = product(normed, w_key).astype(jnp.bfloat16)
    value_own = product(normed, w_value).astype(jnp.bfloat16)
    glob_query = (
        product(glob_normed, w_query)
        .astype(jnp.bfloat16)
        .reshape(group_seqs, GLOBALS, HEADS, HEAD_DIM)
    )
    glob_key = (
        product(glob_normed, w_key)
        .astype(jnp.bfloat16)
        .reshape(group_seqs, GLOBALS, HEADS, HEAD_DIM)
    )
    glob_value = (
        product(glob_normed, w_value)
        .astype(jnp.bfloat16)
        .reshape(group_seqs, GLOBALS, HEADS, HEAD_DIM)
    )
    glob_query_own = own_slot(glob_query)
    glob_key_own = own_slot(glob_key)
    glob_value_own = own_slot(glob_value)
    kv_ext = with_halo(jnp.concatenate([key_own, value_own], axis=1), (("seq", 0),), RADIUS)
    key_ext = kv_ext[:, :D].reshape(ext_count, HEADS, HEAD_DIM)
    value_ext = kv_ext[:, D:].reshape(ext_count, HEADS, HEAD_DIM)
    rank_ext = with_halo(token_ranks, (("seq", 1),), RADIUS)
    rich_q3 = rich_query.reshape(HEAD_DIM, HEADS, 4)
    rich_k3 = rich_key.reshape(HEAD_DIM, HEADS, 4)
    query_heads = query.reshape(tok_count, HEADS, HEAD_DIM)
    a_rows = jnp.einsum("the,ehc->htc", query_heads, rich_q3, preferred_element_type=jnp.float32)
    b_ext = jnp.einsum("the,ehc->htc", key_ext, rich_k3, preferred_element_type=jnp.float32)

    def block_scores():

        def rich_scores(left_rows, right_rows):
            return rich_part(left_rows, right_rows, token_ranks, rank_ext, log_norm)

        rich_vals, rich_back = jax.vjp(rich_scores, a_rows, b_ext)
        raw_scores = (
            jnp.einsum("qhe,khe->hqk", query_heads, key_ext, preferred_element_type=jnp.float32)
            * score_scale
        )
        pos_gap = own_pos[:, None] - ext_pos[None, :]
        key_mask = (jnp.abs(pos_gap) <= RADIUS) & key_valid[None, :]
        scores = jnp.where(key_mask[None], raw_scores + rich_vals, MASKED)
        glob_scores = (
            jnp.einsum(
                "qhe,ghe->hqg", query_heads, glob_key_own, preferred_element_type=jnp.float32
            )
            * score_scale
        )
        return (scores, glob_scores, rich_back, query_heads, key_ext)

    scored = block_scores()
    scores = scored[0]
    glob_scores = scored[1]
    row_top = jnp.maximum(jnp.max(scores, axis=-1), jnp.max(glob_scores, axis=-1))
    row_denom = jnp.sum(jnp.exp(scores - row_top[..., None]), axis=-1) + jnp.sum(
        jnp.exp(glob_scores - row_top[..., None]), axis=-1
    )
    log_total = row_top + jnp.log(row_denom)
    prob_rows = jnp.exp(scores - log_total[..., None]).astype(jnp.bfloat16)
    glob_probs = jnp.exp(glob_scores - log_total[..., None]).astype(jnp.bfloat16)
    attn_block = jnp.einsum(
        "hqk,khe->qhe", prob_rows, value_ext, preferred_element_type=jnp.float32
    ) + jnp.einsum("hqg,ghe->qhe", glob_probs, glob_value_own, preferred_element_type=jnp.float32)
    attn_parts = attn_block.reshape(block_rows, D)
    attn_rows = attn_parts.astype(jnp.bfloat16)
    member_mask = membership[None, :] == jnp.arange(GLOBALS, dtype=jnp.int32)[:, None]
    key_heads = key_ext[RADIUS : RADIUS + tok_count]
    value_heads = value_ext[RADIUS : RADIUS + tok_count]
    member_raw = (
        jnp.einsum("ghe,the->ght", glob_query_own, key_heads, preferred_element_type=jnp.float32)
        * score_scale
    )
    member_scores = jnp.where(member_mask[:, None, :], member_raw, MASKED)
    local_top = jnp.max(member_scores, axis=-1)
    member_exp = jnp.where(
        member_mask[:, None, :], jnp.exp(member_scores - local_top[..., None]), 0.0
    )
    local_sum = jnp.sum(member_exp, axis=-1)
    local_acc = jnp.einsum(
        "ght,the->ghe", member_exp, value_heads.astype(jnp.float32), precision=PRECISE
    )
    slot_top = jnp.where(slot_flag[:, None, None] > 0.5, local_top[None], MASKED)
    slot_sum = to_slots(local_sum)
    slot_acc = to_slots(local_acc)

    def combine_softmax(first_part, second_part):
        top_one, sum_one, acc_one = first_part
        top_two, sum_two, acc_two = second_part
        top_both = jnp.maximum(top_one, top_two)
        scale_one = jnp.exp(top_one - top_both)
        scale_two = jnp.exp(top_two - top_both)
        return (
            top_both,
            sum_one * scale_one + sum_two * scale_two,
            acc_one * scale_one[..., None] + acc_two * scale_two[..., None],
        )

    merged_top, merged_sum, merged_acc = joined(
        (slot_top, slot_sum, slot_acc), "seq", combine_softmax
    )
    self_scores = (
        jnp.einsum("sghe,skhe->sghk", glob_query, glob_key, preferred_element_type=jnp.float32)
        * score_scale
    )
    glob_top = jnp.maximum(merged_top, jnp.max(self_scores, axis=-1))
    self_exp = jnp.exp(self_scores - glob_top[..., None])
    merged_scale = jnp.exp(merged_top - glob_top)
    glob_denom = merged_sum * merged_scale + jnp.sum(self_exp, axis=-1)
    glob_lse = glob_top + jnp.log(glob_denom)
    glob_att_f = (
        merged_acc * merged_scale[..., None]
        + jnp.einsum("sghk,skhe->sghe", self_exp, glob_value.astype(jnp.float32), precision=PRECISE)
    ) / glob_denom[..., None]
    glob_attn = glob_att_f.reshape(group_seqs * GLOBALS, D).astype(jnp.bfloat16)
    y_one = super_rows + product(attn_rows, w_out)
    glob_y_one = glob_in + product(glob_attn, w_out)

    def feed_forward(rows_in):
        normed_two_full, back_two = jax.vjp(layer_norm, rows_in, gain_two, shift_two)
        normed_two = normed_two_full.astype(jnp.bfloat16)
        hidden_pre = product(normed_two, w_up) + bias_up
        hidden_full, gelu_back = jax.vjp(jax.nn.gelu, hidden_pre)
        hidden = hidden_full.astype(jnp.bfloat16)
        result = rows_in + product(hidden, w_down) + bias_down
        return (result, normed_two, hidden, back_two, gelu_back)

    def feed_back(cotangent, normed_two, hidden, back_two, gelu_back):
        cot_full = cotangent.astype(jnp.float32)
        grad_down = product_left(hidden, cotangent)
        grad_bias_d = jnp.sum(cot_full, axis=0)
        d_hidden = product_right(cotangent, w_down)
        d_pre = gelu_back(d_hidden)[0].astype(jnp.bfloat16)
        grad_up = product_left(normed_two, d_pre)
        grad_bias_u = jnp.sum(d_pre.astype(jnp.float32), axis=0)
        d_normed_two = product_right(d_pre, w_up)
        d_rows, grad_gain, grad_shift = back_two(d_normed_two)
        return (
            cot_full + d_rows,
            (grad_gain, grad_shift, grad_up, grad_bias_u, grad_down, grad_bias_d),
        )

    long_ff = feed_forward(y_one)
    glob_ff = feed_forward(glob_y_one)
    out_tokens = long_ff[0].astype(jnp.bfloat16)
    out_global = glob_ff[0].astype(jnp.bfloat16)
    d_y_one, long_mlp = feed_back(cot_tokens, long_ff[1], long_ff[2], long_ff[3], long_ff[4])
    glob_d_y_one, glob_mlp = feed_back(cot_global, glob_ff[1], glob_ff[2], glob_ff[3], glob_ff[4])
    mlp_grads = [
        local_part + first_flag * glob_part for local_part, glob_part in zip(long_mlp, glob_mlp)
    ]
    d_proj = d_y_one.astype(jnp.bfloat16)
    glob_d_proj = glob_d_y_one.astype(jnp.bfloat16)
    grad_out = product_left(attn_rows, d_proj) + first_flag * product_left(glob_attn, glob_d_proj)
    d_attn = product_right(d_proj, w_out).astype(jnp.bfloat16).reshape(tok_count, HEADS, HEAD_DIM)
    glob_d_attn = (
        product_right(glob_d_proj, w_out)
        .astype(jnp.bfloat16)
        .reshape(group_seqs, GLOBALS, HEADS, HEAD_DIM)
    )
    glob_d_attn_own = own_slot(glob_d_attn)
    rich_q3_full = rich_q3.astype(jnp.float32)
    rich_k3_full = rich_k3.astype(jnp.float32)
    d_key_ext = jnp.zeros((ext_count, HEADS, HEAD_DIM), jnp.float32)
    d_value_ext = jnp.zeros((ext_count, HEADS, HEAD_DIM), jnp.float32)
    scores, glob_scores, rich_back, q_part, key_win = block_scores()
    prob_full = jnp.exp(scores - log_total[..., None])
    glob_prob_full = jnp.exp(glob_scores - log_total[..., None])
    d_probs = jnp.einsum("qhe,khe->hqk", d_attn, value_ext, preferred_element_type=jnp.float32)
    glob_d_probs = jnp.einsum(
        "qhe,ghe->hqg", d_attn, glob_value_own, preferred_element_type=jnp.float32
    )
    row_delta = jnp.sum(prob_full * d_probs, axis=-1) + jnp.sum(
        glob_prob_full * glob_d_probs, axis=-1
    )
    d_scores = (prob_full * (d_probs - row_delta[..., None])).astype(jnp.bfloat16)
    glob_d_scores = (glob_prob_full * (glob_d_probs - row_delta[..., None])).astype(jnp.bfloat16)
    query_rich_grad, key_rich_grad = rich_back(d_scores.astype(jnp.float32))
    query_grad = (
        jnp.einsum("hqk,khe->qhe", d_scores, key_win, preferred_element_type=jnp.float32)
        + jnp.einsum(
            "hqg,ghe->qhe", glob_d_scores, glob_key_own, preferred_element_type=jnp.float32
        )
    ) * score_scale + jnp.einsum("hqc,ehc->qhe", query_rich_grad, rich_q3_full, precision=PRECISE)
    key_win_grad = jnp.einsum(
        "hqk,qhe->khe", d_scores, q_part, preferred_element_type=jnp.float32
    ) * score_scale + jnp.einsum("hkc,ehc->khe", key_rich_grad, rich_k3_full, precision=PRECISE)
    value_win_grad = jnp.einsum(
        "hqk,qhe->khe", prob_full.astype(jnp.bfloat16), d_attn, preferred_element_type=jnp.float32
    )
    d_key_ext = d_key_ext.at[0:window].add(key_win_grad)
    d_value_ext = d_value_ext.at[0:window].add(value_win_grad)
    glob_key_grad = (
        jnp.einsum("hqg,qhe->ghe", glob_d_scores, q_part, preferred_element_type=jnp.float32)
        * score_scale
    )
    glob_value_grad = jnp.einsum(
        "hqg,qhe->ghe",
        glob_prob_full.astype(jnp.bfloat16),
        d_attn,
        preferred_element_type=jnp.float32,
    )
    grad_rich_q = jnp.einsum(
        "qhe,hqc->ehc", q_part.astype(jnp.float32), query_rich_grad, precision=PRECISE
    )
    grad_rich_k = jnp.einsum(
        "khe,hkc->ehc", key_win.astype(jnp.float32), key_rich_grad, precision=PRECISE
    )
    query_grads = query_grad.reshape(block_rows, D)
    glob_delta = jnp.sum(glob_d_attn.astype(jnp.float32) * glob_att_f, axis=-1)
    glob_delta_own = own_slot(glob_delta)
    glob_lse_own = own_slot(glob_lse)
    member_probs = jnp.where(
        member_mask[:, None, :], jnp.exp(member_scores - glob_lse_own[..., None]), 0.0
    )
    member_d_probs = jnp.einsum(
        "ghe,the->ght", glob_d_attn_own, value_heads, preferred_element_type=jnp.float32
    )
    member_d_scores = (member_probs * (member_d_probs - glob_delta_own[..., None])).astype(
        jnp.bfloat16
    )
    glob_query_part = (
        jnp.einsum("ght,the->ghe", member_d_scores, key_heads, preferred_element_type=jnp.float32)
        * score_scale
    )
    own_key_extra = (
        jnp.einsum(
            "ght,ghe->the", member_d_scores, glob_query_own, preferred_element_type=jnp.float32
        )
        * score_scale
    )
    own_value_extra = jnp.einsum(
        "ght,ghe->the", member_probs, glob_d_attn_own.astype(jnp.float32), precision=PRECISE
    )
    d_key_ext = d_key_ext.at[RADIUS : RADIUS + tok_count].add(own_key_extra)
    d_value_ext = d_value_ext.at[RADIUS : RADIUS + tok_count].add(own_value_extra)
    grad_rims = jnp.concatenate(
        [d_key_ext.reshape(ext_count, D), d_value_ext.reshape(ext_count, D)], axis=1
    )
    from_above = shifted(grad_rims[:RADIUS].astype(jnp.bfloat16), "seq", -1).astype(jnp.float32)
    from_below = shifted(grad_rims[tok_count + RADIUS :].astype(jnp.bfloat16), "seq", 1).astype(
        jnp.float32
    )
    kv_grad = grad_rims[RADIUS : RADIUS + tok_count]
    kv_grad = kv_grad.at[:RADIUS].add(from_below).at[tok_count - RADIUS :].add(from_above)
    summed_query, summed_key, summed_value = (
        lax.psum(to_slots(glob_query_part).astype(jnp.bfloat16), "seq").astype(jnp.float32),
        lax.psum(to_slots(glob_key_grad).astype(jnp.bfloat16), "seq").astype(jnp.float32),
        lax.psum(to_slots(glob_value_grad).astype(jnp.bfloat16), "seq").astype(jnp.float32),
    )
    self_probs = jnp.exp(self_scores - glob_lse[..., None])
    self_d_probs = jnp.einsum(
        "sghe,skhe->sghk", glob_d_attn, glob_value, preferred_element_type=jnp.float32
    )
    self_d_scores = (self_probs * (self_d_probs - glob_delta[..., None])).astype(jnp.bfloat16)
    glob_rows_total = group_seqs * GLOBALS
    glob_d_query = (
        (
            summed_query
            + jnp.einsum(
                "sghk,skhe->sghe", self_d_scores, glob_key, preferred_element_type=jnp.float32
            )
            * score_scale
        )
        .astype(jnp.bfloat16)
        .reshape(glob_rows_total, D)
    )
    glob_d_key = (
        (
            summed_key
            + jnp.einsum(
                "sghk,sghe->skhe", self_d_scores, glob_query, preferred_element_type=jnp.float32
            )
            * score_scale
        )
        .astype(jnp.bfloat16)
        .reshape(glob_rows_total, D)
    )
    glob_d_value = (
        (
            summed_value
            + jnp.einsum(
                "sghk,sghe->skhe", self_probs, glob_d_attn.astype(jnp.float32), precision=PRECISE
            )
        )
        .astype(jnp.bfloat16)
        .reshape(glob_rows_total, D)
    )
    d_query = query_grads.astype(jnp.bfloat16)
    d_key = kv_grad[:, :D].astype(jnp.bfloat16)
    d_value = kv_grad[:, D:].astype(jnp.bfloat16)
    grad_query = product_left(normed, d_query) + first_flag * product_left(
        glob_normed, glob_d_query
    )
    grad_key = product_left(normed, d_key) + first_flag * product_left(glob_normed, glob_d_key)
    grad_value = product_left(normed, d_value) + first_flag * product_left(
        glob_normed, glob_d_value
    )
    d_normed = (
        product_right(d_query, w_query)
        + product_right(d_key, w_key)
        + product_right(d_value, w_value)
    )
    glob_d_normed = (
        product_right(glob_d_query, w_query)
        + product_right(glob_d_key, w_key)
        + product_right(glob_d_value, w_value)
    )
    d_super_norm, grad_gain_one, grad_shift_one = norm_back(d_normed)
    d_super = d_y_one + d_super_norm
    glob_d_norm, glob_gain_one, glob_shift_one = glob_norm_back(glob_d_normed)
    grad_global = glob_d_y_one + glob_d_norm
    grad_gain_one = grad_gain_one + first_flag * glob_gain_one
    grad_shift_one = grad_shift_one + first_flag * glob_shift_one
    d_graph_pre = graph_back(d_super)[0].astype(jnp.bfloat16)
    grad_graph = product_left(agg_low, d_graph_pre)
    d_agg = product_right(d_graph_pre, w_graph) / NEIGH
    d_token_ext = (
        jnp.zeros((ext_count, D), jnp.float32).at[flat_index].add(jnp.repeat(d_agg, NEIGH, axis=0))
    )
    d_token_ext = jnp.where(key_valid[:, None], d_token_ext, 0.0)
    token_above = shifted(d_token_ext[:RADIUS].astype(jnp.bfloat16), "seq", -1).astype(jnp.float32)
    token_below = shifted(d_token_ext[tok_count + RADIUS :].astype(jnp.bfloat16), "seq", 1).astype(
        jnp.float32
    )
    own_grad = (
        d_token_ext[RADIUS : RADIUS + tok_count]
        .at[:RADIUS]
        .add(token_below)
        .at[tok_count - RADIUS :]
        .add(token_above)
    )
    grad_tokens = d_super + own_grad
    weight_grads = (
        grad_graph,
        grad_gain_one,
        grad_shift_one,
        grad_query,
        grad_key,
        grad_value,
        grad_rich_q.reshape(HEAD_DIM, 4 * HEADS),
        grad_rich_k.reshape(HEAD_DIM, 4 * HEADS),
        grad_out,
        mlp_grads[0],
        mlp_grads[1],
        mlp_grads[2],
        mlp_grads[3],
        mlp_grads[4],
        mlp_grads[5],
    )
    pieces = [weight_grad.reshape(seq_count, -1) for weight_grad in weight_grads]
    packed = jnp.concatenate(pieces, axis=1)
    group_count = lax.axis_size("grp")
    received = lax.all_to_all(
        packed.astype(jnp.bfloat16), "seq", split_axis=0, concat_axis=0, tiled=True
    ).astype(packed.dtype)
    group_total = jnp.sum(received, axis=0).reshape(group_count, -1)
    crossed = lax.all_to_all(
        group_total.astype(jnp.bfloat16), "grp", split_axis=0, concat_axis=0, tiled=True
    ).astype(group_total.dtype)
    final_part = jnp.sum(crossed, axis=0)
    flat_sum = lax.all_gather(final_part.astype(jnp.bfloat16), "grp", axis=0, tiled=True).astype(
        final_part.dtype
    )
    results = []
    offset = 0
    for weight_grad in weight_grads:
        part_len = weight_grad.size // seq_count
        results.append(
            flat_sum[offset : offset + part_len].reshape(
                (weight_grad.shape[0] // seq_count,) + weight_grad.shape[1:]
            )
        )
        offset = offset + part_len
    return (
        out_tokens,
        out_global,
        grad_tokens,
        grad_global,
        results[0],
        results[1],
        results[2],
        results[3],
        results[4],
        results[5],
        results[6],
        results[7],
        results[8],
        results[9],
        results[10],
        results[11],
        results[12],
        results[13],
        results[14],
    )


def solution(mesh):
    return jax.shard_map(
        local,
        mesh=mesh,
        in_specs=(
            P(("grp", "seq"), None),
            P("grp", None),
            P(("grp", "seq"), None),
            P(None, ("grp", "seq")),
            P(("grp", "seq")),
            P(),
            P(),
            P(),
            P(),
            P(),
            P(),
            P(),
            P(),
            P(),
            P(),
            P(),
            P(),
            P(),
            P(),
            P(),
            P(("grp", "seq"), None),
            P("grp", None),
        ),
        out_specs=(
            P(("grp", "seq"), None),
            P("grp", None),
            P(("grp", "seq"), None),
            P("grp", None),
            P("seq", None),
            P("seq"),
            P("seq"),
            P("seq", None),
            P("seq", None),
            P("seq", None),
            P("seq", None),
            P("seq", None),
            P("seq", None),
            P("seq"),
            P("seq"),
            P("seq", None),
            P("seq"),
            P("seq", None),
            P("seq"),
        ),
        check_vma=False,
    )
```

profile of v0, /device:TPU:0, one launch (start us, length us, event | category | flops | bytes accessed | tf_op | source)
XLA Modules:
  0.0 1249.1 jit_solution(6324320230209957025)
XLA Ops:
  11.8 5.1 collective-permute-start.4
  30.6 5.3 fusion.232
  47.7 5.5 gather_fusion
  60.6 4.5 collective-permute-start.2
  69.8 12.3 all-gather.2
  82.2 5.2 all-gather.4
  87.4 5.2 all-gather.3
  99.9 5.8 convert_reduce_fusion.2
  125.2 9.5 fusion.223
  143.1 6.5 convert_reduce_fusion.1
  163.9 5.9 fusion.18
  171.4 7.8 fusion.52
  181.2 5.2 fusion.193
  216.0 4.0 concatenate.105
  221.4 7.4 add_convert_fusion.1
  228.8 8.0 concatenate.108
  239.0 3.6 add_convert_fusion
  242.6 7.0 concatenate.110
  250.9 34.1 %all-reduce.15.cloned.1.call-done = (bf16[1,64,12,64]{1,3,2,0:T(8,128)(2,1)}, bf16[1,64,12,64]{1,3,2,0:T(8,128)(2,1)}, bf16[1,64,12,64]{1,3,2,0:T(8,128)(2,1)}) async-done(((bf16[1,64,12,64]{1,3,2,0:T(8,128)(2,1)}, bf16[1,64,12,64]{1,3,2,0:T(8,128)(2,1)}, bf16[1,64,12,64]{1,3,2,0:T(8,128)(2,1)}), (bf16[1,64,12,64]{1,3,2,0:T(8,128)(2,1)}, bf16[1,64,12,64]{1,3,2,0:T(8,128)(2,1)}, ...) | async-done | bytes 294928 | tf_op jit(solution)/shard_map/psum | solution.py:415
  297.1 4.2 concatenate.100
  310.4 5.2 constant_dynamic-update-slice_fusion.13
  317.3 3.9 concatenate.101
  322.8 4.0 concatenate.102
  330.1 3.6 constant_dynamic-update-slice_fusion.12
  333.7 3.5 constant_dynamic-update-slice_fusion.11
  337.2 3.6 constant_dynamic-update-slice_fusion.10
  342.0 3.5 constant_dynamic-update-slice_fusion.7
  348.8 12.9 %constant_dynamic-update-slice_fusion.6 = bf16[4,1,1920192]{2,1,0:T(2,128)(2,1)} fusion(bf16[4,1,1920192]{2,1,0:T(2,128)(2,1)} %dynamic-update-slice.29, bf16[4,1,589824]{2,1,0:T(2,128)(2,1)} %concatenate.108), kind=kLoop, calls=%fused_computation.331 | loop fusion | bytes 18874368
  362.4 11.1 constant_dynamic-update-slice_fusion.4
  374.5 92.7 %reduce.31 = bf16[4,1920192]{1,0:T(4,128)(2,1)} reduce(bf16[4,1,1920192]{2,1,0:T(2,128)(2,1)} %constant_dynamic-update-slice_fusion.3, bf16[]{:T(256)} %broadcast.982), dimensions={1}, to_apply=%constant_dynamic-update-slice_fusion.3.reduce_sub_computation | reduce | bytes 30723074 | tf_op jit(solution)/shard_map/concatenate | solution.py:520
  467.2 70.3 %reshape.1545 = bf16[4,2,960096]{2,1,0:T(2,128)(2,1)} reshape(bf16[4,1920192]{1,0:T(4,128)(2,1)} %reduce.31) | data formatting | bytes 30723072
  537.5 178.4 %all_to_all.12 = bf16[4,2,960096]{2,1,0:T(2,128)(2,1)} all-to-all(bf16[4,2,960096]{2,1,0:T(2,128)(2,1)} %reshape.1545), channel_id=1, replica_groups=mesh['grp'=8,'seq'=4] {'seq'}, dimensions={0} | all-to-all | bytes 30723072 | tf_op jit(solution)/shard_map/all_to_all | solution.py:522
  715.9 54.1 %reshape.1546 = bf16[4,1,1920192]{2,1,0:T(2,128)(2,1)} reshape(bf16[4,2,960096]{2,1,0:T(2,128)(2,1)} %all_to_all.12) | data formatting | bytes 30723072
  769.9 84.1 %reduce_sum.563 = bf16[1920192]{0:T(1024)(128)(2,1)} reduce(bf16[4,1,1920192]{2,1,0:T(2,128)(2,1)} %reshape.1546, bf16[]{:T(256)} %constant.431.clone.1), dimensions={0,1}, to_apply=%region_54.56 | reduce | flops 5760576 | bytes 19201922 | tf_op jit(solution)/shard_map/reduce_sum | solution.py:525
  854.0 9.0 convert_element_type.529
  863.0 83.0 %reduce.32 = bf16[8,240024]{1,0:T(8,128)(2,1)} reduce(bf16[8,1,240024]{2,1,0:T(2,128)(2,1)} %convert_element_type.529, bf16[]{:T(256)} %broadcast.982), dimensions={1}, to_apply=%convert_element_type.529.reduce_sub_computation | reduce | bytes 7680770 | tf_op jit(solution)/shard_map/convert_element_type | solution.py:527
  946.0 7.4 reshape.1547
  953.3 5.6 all-to-all-start.1
  960.3 84.6 %all-to-all-done.1 = bf16[8,2,120012]{2,1,0:T(2,128)(2,1)} async-done(((bf16[8,2,120012]{2,1,0:T(2,128)(2,1)}), bf16[8,2,120012]{2,1,0:T(2,128)(2,1)}, u32[]{:S(2)}, u32[]{:S(2)}) %all-to-all-start.1) | async-done | bytes 3840416 | tf_op jit(solution)/shard_map/all_to_all | solution.py:526
  1044.8 10.8 reshape.1548
  1055.7 11.4 reduce_sum.564
  1069.2 8.2 dynamic-update-slice.18
  1077.4 4.1 fusion.108
  1082.1 7.9 scatter_custom_fusion
  1093.2 4.1 fusion.90
  1098.2 125.1 %all-reduce.13.cloned.1.call-done = bf16[1920192]{0:T(1024)(128)(2,1)} async-done(((bf16[1920192]{0:T(1024)(128)(2,1)}), bf16[1920192]{0:T(1024)(128)(2,1)}) %all-reduce.13.cloned.1.call-update) | async-done | bytes 3840400
  1223.4 3.3 fusion.215
  1226.7 3.2 reshape.1487
  (716 shorter events, 182.7 us)
Async XLA Ops:
  7.2 20.7 %copy-start = (bf16[768,768]{1,0:T(8,128)(2,1)S(1)}, bf16[768,768]{1,0:T(8,128)(2,1)}, u32[]{:S(2)}) copy-start(bf16[768,768]{1,0:T(8,128)(2,1)} %param.63) | copy-start | bytes 3538948
  7.2 22.7 %copy-start.9 = (bf16[64,768]{1,0:T(8,128)(2,1)S(1)}, bf16[64,768]{1,0:T(8,128)(2,1)}, u32[]{:S(2)}) copy-start(bf16[64,768]{1,0:T(8,128)(2,1)} %param.54) | copy-start | bytes 294916
  7.2 22.7 %copy-start.122 = (f32[768]{0:T(1024)S(1)}, f32[768]{0:T(1024)}, u32[]{:S(2)}) copy-start(f32[768]{0:T(1024)} %param.59) | copy-start | bytes 9220
  7.2 22.7 %copy-start.128 = (f32[768]{0:T(1024)S(1)}, f32[768]{0:T(1024)}, u32[]{:S(2)}) copy-start(f32[768]{0:T(1024)} %param.60) | copy-start | bytes 9220
  7.2 22.7 %copy-start.5 = (bf16[768,768]{1,0:T(8,128)(2,1)S(1)}, bf16[768,768]{1,0:T(8,128)(2,1)}, u32[]{:S(2)}) copy-start(bf16[768,768]{1,0:T(8,128)(2,1)} %param.61) | copy-start | bytes 3538948
  7.3 277.7 %all-reduce.15.cloned.1.call-start = ((), (), s32[]{:S(2)}) async-start(), calls=%async_computation.3 | async-start | bytes 1179648 | tf_op jit(solution)/shard_map/psum | solution.py:415
  7.3 39.1 %collective-permute-start = (bf16[128,768]{1,0:T(8,128)(2,1)}, bf16[128,768]{1,0:T(8,128)(2,1)}, u32[]{:S(2)}, u32[]{:S(2)}) collective-permute-start(bf16[128,768]{1,0:T(8,128)(2,1)} %param.53), channel_id=1, source_target_pairs={{0,1},{1,2},{2,3},{4,5},{5,6},{6,7},{8,9},{9,10},{10,11},{12,13},{... | collective-permute-start | bytes 589832 | tf_op jit(solution)/shard_map/ppermute | solution.py:30
  10.5 36.0 %collective-permute-start.1 = (bf16[128,768]{1,0:T(8,128)(2,1)}, bf16[128,768]{1,0:T(8,128)(2,1)}, u32[]{:S(2)}, u32[]{:S(2)}) collective-permute-start(bf16[128,768]{1,0:T(8,128)(2,1)} %param.53), channel_id=1, source_target_pairs={{1,0},{2,1},{3,2},{5,4},{6,5},{7,6},{9,8},{10,9},{11,10},{13,12},{... | collective-permute-start | bytes 589832 | tf_op jit(solution)/shard_map/ppermute | solution.py:32
  11.8 29.9 %collective-permute-start.4 = (s32[2,128]{1,0:T(2,128)}, s32[2,128]{1,0:T(2,128)}, u32[]{:S(2)}, u32[]{:S(2)}) collective-permute-start(s32[2,128]{1,0:T(2,128)} %param.56), channel_id=1, source_target_pairs={{0,1},{1,2},{2,3},{4,5},{5,6},{6,7},{8,9},{9,10},{10,11},{12,13},{... | collective-permute-start | bytes 3080 | tf_op jit(solution)/shard_map/ppermute | solution.py:30
  16.8 25.5 %collective-permute-start.5 = (s32[2,128]{1,0:T(2,128)}, s32[2,128]{1,0:T(2,128)}, u32[]{:S(2)}, u32[]{:S(2)}) collective-permute-start(s32[2,128]{1,0:T(2,128)} %param.56), channel_id=1, source_target_pairs={{1,0},{2,1},{3,2},{5,4},{6,5},{7,6},{9,8},{10,9},{11,10},{13,12},{... | collective-permute-start | bytes 3080 | tf_op jit(solution)/shard_map/ppermute | solution.py:32
  27.9 10.5 copy-start.59
  30.6 38.0 %copy-start.125 = (pred[64,128]{1,0:T(8,128)(4,1)}, pred[64,128]{1,0:T(8,128)(4,1)S(1)}, u32[]{:S(2)}) copy-start(pred[64,128]{1,0:T(8,128)(4,1)S(1)} %iota_compare_fusion) | copy-start | bytes 24580
  39.3 80.1 %copy-start.45 = (f32[1,64,12,64]{1,3,2,0:T(8,128)}, f32[1,64,12,64]{1,3,2,0:T(8,128)S(1)}, u32[]{:S(2)}) copy-start(f32[1,64,12,64]{1,3,2,0:T(8,128)S(1)} %get-tuple-element.505) | copy-start | bytes 589828
  59.8 9.7 copy-start.82
  60.6 61.3 %collective-permute-start.2 = (bf16[128,1536]{1,0:T(8,128)(2,1)}, bf16[128,1536]{1,0:T(8,128)(2,1)}, u32[]{:S(2)}, u32[]{:S(2)}) collective-permute-start(bf16[128,1536]{1,0:T(8,128)(2,1)} %pad_maximum_fusion.2), channel_id=1, source_target_pairs={{0,1},{1,2},{2,3},{4,5},{5,6},{6,7},{8,9},{9,10},{10,11},{12,13},{... | collective-permute-start | bytes 1179656 | tf_op jit(solution)/shard_map/ppermute | solution.py:30
  65.1 56.8 %collective-permute-start.3 = (bf16[128,1536]{1,0:T(8,128)(2,1)}, bf16[128,1536]{1,0:T(8,128)(2,1)}, u32[]{:S(2)}, u32[]{:S(2)}) collective-permute-start(bf16[128,1536]{1,0:T(8,128)(2,1)} %pad_maximum_fusion.2), channel_id=1, source_target_pairs={{1,0},{2,1},{3,2},{5,4},{6,5},{7,6},{9,8},{10,9},{11,10},{13,12},{... | collective-permute-start | bytes 1179656 | tf_op jit(solution)/shard_map/ppermute | solution.py:32
  110.1 9.3 copy-start.84
  111.1 9.1 copy-start.60
  112.3 9.6 copy-start.42
  124.7 10.0 copy-start.160
  124.7 10.0 copy-start.141
  124.7 10.0 copy-start.162
  124.7 10.0 copy-start.164
  125.2 9.5 copy-start.152
  125.2 9.6 copy-start.12
  142.4 9.6 copy-start.20
  142.4 9.6 copy-start.176
  143.1 8.9 copy-start.182
  171.4 9.3 copy-start.100
  171.4 9.3 copy-start.104
  198.1 105.3 %collective-permute-start.6 = (bf16[128,1536]{0,1:T(8,128)(2,1)}, bf16[128,1536]{0,1:T(8,128)(2,1)}, u32[]{:S(2)}, u32[]{:S(2)}) collective-permute-start(bf16[128,1536]{0,1:T(8,128)(2,1)} %get-tuple-element.470), channel_id=1, source_target_pairs={{0,1},{1,2},{2,3},{4,5},{5,6},{6,7},{8,9},{9,10},{10,11},{12,13},{... | collective-permute-start | bytes 1179656 | tf_op jit(solution)/shard_map/ppermute | solution.py:57
  201.0 102.3 %collective-permute-start.7 = (bf16[128,1536]{0,1:T(8,128)(2,1)}, bf16[128,1536]{0,1:T(8,128)(2,1)}, u32[]{:S(2)}, u32[]{:S(2)}) collective-permute-start(bf16[128,1536]{0,1:T(8,128)(2,1)} %get-tuple-element.471), channel_id=1, source_target_pairs={{1,0},{2,1},{3,2},{5,4},{6,5},{7,6},{9,8},{10,9},{11,10},{13,12},{... | collective-permute-start | bytes 1179656 | tf_op jit(solution)/shard_map/ppermute | solution.py:57
  249.6 35.4 %copy-start.46 = (f32[1,64,12,64]{1,3,2,0:T(8,128)S(1)}, f32[1,64,12,64]{1,3,2,0:T(8,128)}, u32[]{:S(2)}) copy-start(f32[1,64,12,64]{1,3,2,0:T(8,128)} %copy-done.45) | copy-start | bytes 589828
  249.6 35.4 %copy-start.97 = (bf16[64,12,64]{0,2,1:T(8,128)(2,1)S(1)}, bf16[64,12,64]{0,2,1:T(8,128)(2,1)}, u32[]{:S(2)}) copy-start(bf16[64,12,64]{0,2,1:T(8,128)(2,1)} %copy.207) | copy-start | bytes 294916
  249.6 36.9 %copy-start.65 = (bf16[64,768]{0,1:T(8,128)(2,1)S(1)}, bf16[64,768]{0,1:T(8,128)(2,1)}, u32[]{:S(2)}) copy-start(bf16[64,768]{0,1:T(8,128)(2,1)} %copy-done.62) | copy-start | bytes 294916
  249.6 36.9 %copy-start.98 = (bf16[64,12,64]{0,2,1:T(8,128)(2,1)S(1)}, bf16[64,12,64]{0,2,1:T(8,128)(2,1)}, u32[]{:S(2)}) copy-start(bf16[64,12,64]{0,2,1:T(8,128)(2,1)} %fusion.106) | copy-start | bytes 294916
  250.9 38.7 %copy-start.129 = (f32[768]{0:T(1024)S(1)}, f32[768]{0:T(1024)}, u32[]{:S(2)}) copy-start(f32[768]{0:T(1024)} %param.60) | copy-start | bytes 9220
  250.9 38.7 %copy-start.144 = (f32[64]{0:T(128)S(1)}, f32[64]{0:T(128)}, u32[]{:S(2)}) copy-start(f32[64]{0:T(128)} %copy-done.143) | copy-start | bytes 772
  250.9 38.7 %copy-start.155 = (f32[64]{0:T(128)S(1)}, f32[64]{0:T(128)}, u32[]{:S(2)}) copy-start(f32[64]{0:T(128)} %copy-done.154) | copy-start | bytes 772
  342.0 20.3 %slice-start = ((s8[9437184]{0:T(1024)(128)(4,1)}), s8[1048576]{0:T(1024)(128)(4,1)S(1)}, s32[]{:S(2)}) async-start(s8[9437184]{0:T(1024)(128)(4,1)} %bitcast.330), calls=%async_computation.4 | async-start | bytes 2097152
  348.8 12.9 %copy-start.151 = (bf16[4,1,768]{2,1,0:T(2,128)(2,1)S(1)}, bf16[4,1,768]{2,1,0:T(2,128)(2,1)}, u32[]{:S(2)}) copy-start(bf16[4,1,768]{2,1,0:T(2,128)(2,1)} %concatenate.109) | copy-start | bytes 18436
  348.8 13.5 %slice-start.1 = ((s8[9437184]{0:T(1024)(128)(4,1)}), s8[4194304]{0:T(1024)(128)(4,1)S(1)}, s32[]{:S(2)}) async-start(s8[9437184]{0:T(1024)(128)(4,1)} %bitcast.330), calls=%async_computation.5 | async-start | bytes 8388608
  348.8 13.5 %slice-start.2 = ((s8[9437184]{0:T(1024)(128)(4,1)}), s8[4194304]{0:T(1024)(128)(4,1)S(1)}, s32[]{:S(2)}) async-start(s8[9437184]{0:T(1024)(128)(4,1)} %bitcast.330), calls=%async_computation.6 | async-start | bytes 8388608
  953.3 91.5 %all-to-all-start.1 = ((bf16[8,2,120012]{2,1,0:T(2,128)(2,1)}), bf16[8,2,120012]{2,1,0:T(2,128)(2,1)}, u32[]{:S(2)}, u32[]{:S(2)}) async-start(bf16[8,2,120012]{2,1,0:T(2,128)(2,1)} %reshape.1547), calls=%async_computation.1 | async-start | bytes 7684096 | tf_op jit(solution)/shard_map/all_to_all | solution.py:526
  959.0 264.4 %all-reduce.13.cloned.1.call-start = ((), (), s32[]{:S(2)}) async-start(), calls=%async_computation.2 | async-start | bytes 7684096
  1082.1 11.1 copy-start.22
  1090.2 7.0 collective-permute-start.8
  1091.7 5.6 collective-permute-start.9
  (193 other events, 752.0 us)
Sparse Core Ops, SparseCore 0:
  249.7 35.1 all-reduce.14
  1077.5 145.7 all-reduce.12
where the time goes:
time: 1260 us; the launch traced here: 1250 us
  other arithmetic  324 us (26%)
  local copies, waits for them, and re-layouts  311 us (25%)
  waiting for transfers between devices  244 us (19%)
  blocking collectives  201 us (16%)
  matrix products  122 us (10%)
  starting transfers between devices  29.4 us (2%)
  between operations  18.2 us (1%)
    unnamed x492, local copies, waits for them, and re-layouts  220 us
    all_to_all x1, blocking collectives, local(): lax.all_to_all(packed.astype(jnp.bfloat16), 'seq', split_axis=0, concat_a...  178 us
    unnamed x3, waiting for transfers between devices  125 us
    concatenate x1, other arithmetic, local(): packed = jnp.concatenate(pieces, axis=1)  92.7 us
    all_to_all x1, waiting for transfers between devices, local(): lax.all_to_all(group_total.astype(jnp.bfloat16), 'grp', split_axis=0, con...  84.6 us
    reduce_sum x1, other arithmetic, local(): group_total = jnp.sum(received, axis=0).reshape(group_count, -1)  84.1 us
    convert_element_type x1, other arithmetic, local(): group_total.astype(jnp.bfloat16)  83 us
    concatenate x17, local copies, waits for them, and re-layouts, local(): packed = jnp.concatenate(pieces, axis=1)  39.8 us
  transfers between devices with their start and end apart: 13, of which 3 were waited for; matrix products, arithmetic and copies ran while one was open for 11% of the time, Pallas kernels for 0%

commit v1 on v0

--- a/solution.py
+++ b/solution.py
@@ -3,6 +3,8 @@
 import jax
 import jax.numpy as jnp
 from jax import lax
+from jax.experimental import pallas as pl
+from jax.experimental.pallas import tpu as pltpu
 from jax.sharding import PartitionSpec as P
 
 D = 768
@@ -563,9 +565,690 @@
     )
 
 
+SEQ_WAYS = 4
+GRP_WAYS = 8
+OWN_HEADS = HEADS // SEQ_WAYS
+OWN = D // SEQ_WAYS
+FF = 3072
+FF_OWN = FF // SEQ_WAYS
+TOK = 128
+ROWS = SEQ_WAYS * TOK
+ALL = ROWS + GLOBALS
+GLOB_OWN = GLOBALS // SEQ_WAYS
+CHUNK = TOK + GLOB_OWN
+WIN = TOK + 2 * RADIUS
+PAD = ROWS + 2 * RADIUS
+BF = jnp.bfloat16
+F32 = jnp.float32
+GELU_SCALE = math.sqrt(2.0 / math.pi)
+GELU_CUBE = 0.044715
+LOG_NORM = math.log(1.0 + ROWS)
+SCORE_SCALE = 1.0 / math.sqrt(HEAD_DIM)
+CORE_SWAP = [(0, 1), (1, 0), (2, 3), (3, 2)]
+Y_SWAP = [(0, 2), (2, 0), (1, 3), (3, 1)]
+X_SWAP = [(g, g ^ 1) for g in range(GRP_WAYS)]
+Z_NEAR = [(g, g ^ 2) for g in range(GRP_WAYS)]
+Z_FAR = [(g, g ^ 4) for g in range(GRP_WAYS)]
+
+
+def nn(left, right):
+    return lax.dot_general(left, right, (((1,), (0,)), ((), ())), preferred_element_type=F32)
+
+
+def nt(left, right):
+    return lax.dot_general(left, right, (((1,), (1,)), ((), ())), preferred_element_type=F32)
+
+
+def tn(left, right):
+    return lax.dot_general(left, right, (((0,), (0,)), ((), ())), preferred_element_type=F32)
+
+
+def pick(stacked, index):
+    return lax.dynamic_index_in_dim(stacked, index, 0, keepdims=False)
+
+
+def gather_seq(block):
+    across = lax.ppermute(block, "seq", Y_SWAP)
+    beside = lax.ppermute(block, "seq", CORE_SWAP)
+    diagonal = lax.ppermute(across, "seq", CORE_SWAP)
+    return [block, beside, across, diagonal]
+
+
+def scatter_seq(chunks):
+    me = lax.axis_index("seq")
+    core, y = me % 2, me // 2
+    grid = chunks.reshape((2, 2) + chunks.shape[1:])
+    sent = lax.dynamic_index_in_dim(grid, 1 - core, 1, keepdims=False)
+    kept = lax.dynamic_index_in_dim(grid, core, 1, keepdims=False)
+    half = kept.astype(F32) + lax.ppermute(sent, "seq", CORE_SWAP).astype(F32)
+    far = lax.ppermute(pick(half, 1 - y).astype(BF), "seq", Y_SWAP)
+    return pick(half, y) + far.astype(F32)
+
+
+def turn_seq(chunks):
+    me = lax.axis_index("seq")
+    core, y = me % 2, me // 2
+    grid = chunks.reshape((2, 2) + chunks.shape[1:])
+    kept = lax.dynamic_index_in_dim(grid, core, 1, keepdims=False)
+    sent = lax.dynamic_index_in_dim(grid, 1 - core, 1, keepdims=False)
+    came = lax.ppermute(sent, "seq", CORE_SWAP)
+    low = jnp.where(core == 0, kept, came)
+    high = jnp.where(core == 0, came, kept)
+    pair = jnp.stack([low, high], axis=1)
+    far = lax.ppermute(pick(pair, 1 - y), "seq", Y_SWAP)
+    near = pick(pair, y)
+    return jnp.concatenate([jnp.where(y == 0, near, far), jnp.where(y == 0, far, near)], axis=0)
+
+
+def reduce_grp(chunks):
+    me = lax.axis_index("grp")
+    x, z_low, z_high = me % 2, (me // 2) % 2, me // 4
+    grid = chunks.reshape((4, 2) + chunks.shape[1:])
+    sent = lax.dynamic_index_in_dim(grid, 1 - x, 1, keepdims=False)
+    kept = lax.dynamic_index_in_dim(grid, x, 1, keepdims=False)
+    part = (kept.astype(F32) + lax.ppermute(sent, "grp", X_SWAP).astype(F32)).astype(BF)
+    part = part.reshape((2, 2) + part.shape[1:])
+    sent = lax.dynamic_index_in_dim(part, 1 - z_low, 1, keepdims=False)
+    kept = lax.dynamic_index_in_dim(part, z_low, 1, keepdims=False)
+    part = (kept.astype(F32) + lax.ppermute(sent, "grp", Z_NEAR).astype(F32)).astype(BF)
+    came = lax.ppermute(pick(part, 1 - z_high), "grp", Z_FAR)
+    return pick(part, z_high).astype(F32) + came.astype(F32)
+
+
+def gather_grp(block):
+    me = lax.axis_index("grp")
+    x, z_low, z_high = me % 2, (me // 2) % 2, me // 4
+
+    def both(flag, mine, other, axis):
+        low = jnp.where(flag == 0, mine, other)
+        high = jnp.where(flag == 0, other, mine)
+        return jnp.stack([low, high], axis=axis)
+
+    block = block.astype(BF)
+    held = both(z_high, block, lax.ppermute(block, "grp", Z_FAR), 0)
+    held = both(z_low, held, lax.ppermute(held, "grp", Z_NEAR), 1)
+    held = both(x, held, lax.ppermute(held, "grp", X_SWAP), 2)
+    return held.reshape((GRP_WAYS,) + block.shape)
+
+
+def row_stats(rows_in):
+    centred = rows_in - jnp.mean(rows_in, axis=-1, keepdims=True)
+    scale = lax.rsqrt(jnp.mean(centred * centred, axis=-1, keepdims=True) + EPSILON)
+    return centred * scale, scale
+
+
+def norm_back(cotangent, gain, rows_in):
+    hat, scale = row_stats(rows_in)
+    scaled = cotangent * gain
+    back = scale * (
+        scaled
+        - jnp.mean(scaled, axis=-1, keepdims=True)
+        - hat * jnp.mean(scaled * hat, axis=-1, keepdims=True)
+    )
+    return (
+        back,
+        jnp.sum(cotangent * hat, axis=0, keepdims=True),
+        jnp.sum(cotangent, axis=0, keepdims=True),
+    )
+
+
+def gelu_parts(pre):
+    square = pre * pre
+    bent = jnp.tanh(GELU_SCALE * pre * (1.0 + GELU_CUBE * square))
+    half = 0.5 * (1.0 + bent)
+    slope = half + 0.5 * pre * (1.0 - bent * bent) * (
+        GELU_SCALE * (1.0 + 3.0 * GELU_CUBE * square)
+    )
+    return pre * half, slope
+
+
+def counts_of(neigh, first, width):
+    spots = lax.broadcasted_iota(jnp.int32, (neigh.shape[0], width), 1) + first
+    total = jnp.zeros((neigh.shape[0], width), F32)
+    for k in range(NEIGH):
+        total = total + jnp.where(neigh[:, k : k + 1] == spots, 1.0, 0.0)
+    return total.astype(BF)
+
+
+def graph_kernel(
+    me_ref, tok_a, tok_b, tok_c, tok_d, int_a, int_b, int_c, int_d, glob_ref, w_graph_ref,
+    w_qkv_ref, gain_ref, shift_ref,
+    agg_ref, pre_ref, super_ref, normed_ref, qkv_ref, meta_col_ref, meta_row_ref, padded,
+):
+    me = me_ref[0]
+    padded[:RADIUS] = jnp.zeros((RADIUS, D), BF)
+    padded[RADIUS + ROWS :] = jnp.zeros((RADIUS, D), BF)
+    starts = [pl.multiple_of((me ^ k) * TOK, TOK) for k in range(SEQ_WAYS)]
+    for start, tok in zip(starts, (tok_a, tok_b, tok_c, tok_d)):
+        padded[pl.ds(start + RADIUS, TOK)] = tok[...]
+    for start, ints in zip(starts, (int_a, int_b, int_c, int_d)):
+        values = ints[...]
+        floats = values.astype(F32)
+        meta_col_ref[pl.ds(start, TOK)] = floats
+        meta_row_ref[:, pl.ds(start, TOK)] = floats.T[:16]
+        counts = counts_of(values, 0, WIN)
+        mean = nn(counts, padded[pl.ds(start, WIN)]) * (1.0 / NEIGH)
+        agg_ref[pl.ds(start, TOK)] = mean.astype(BF)
+    gain, shift = gain_ref[...], shift_ref[...]
+    for low in range(0, ROWS, 256):
+        rows = slice(low, low + 256)
+        pre = nn(agg_ref[rows], w_graph_ref[...])
+        pre_ref[rows] = pre
+        tokens = padded[RADIUS + low : RADIUS + low + 256].astype(F32)
+        super_rows = tokens + gelu_parts(pre)[0]
+        super_ref[rows] = super_rows
+        normed_ref[rows] = (row_stats(super_rows)[0] * gain + shift).astype(BF)
+    glob_hat = row_stats(glob_ref[...].astype(F32))[0]
+    normed_ref[ROWS:] = (glob_hat * gain + shift).astype(BF)
+    projected = nn(normed_ref[...], w_qkv_ref[...]).astype(BF)
+    for part in range(3 * OWN_HEADS):
+        qkv_ref[part] = projected[:, part * HEAD_DIM : (part + 1) * HEAD_DIM]
+
+
+def pair_terms(meta_col, meta_row):
+    terms = []
+    for c in range(2):
+        gap = meta_col[:, 8 + c : 9 + c] - meta_row[8 + c : 9 + c]
+        distance = jnp.log(1.0 + jnp.abs(gap)) * (1.0 / LOG_NORM)
+        terms.append((gap < 0.0, distance))
+    return terms
+
+
+def attend_kernel(
+    qkv_ref, meta_col_ref, meta_row_ref, rich_q_ref, rich_k_ref,
+    attn_ref, prob_ref, glob_prob_ref, member_ref, self_ref, glob_att_ref,
+    keys, values, key_rich, meta_pad,
+):
+    edge = jnp.zeros((OWN_HEADS, RADIUS, HEAD_DIM), BF)
+    for held, first in ((keys, OWN_HEADS), (values, 2 * OWN_HEADS)):
+        held[:, :RADIUS] = edge
+        held[:, RADIUS + ROWS :] = edge
+        held[:, RADIUS : RADIUS + ROWS] = qkv_ref[first : first + OWN_HEADS, :ROWS]
+    meta_pad[...] = jnp.zeros((16, PAD), F32)
+    meta_pad[:, RADIUS : RADIUS + ROWS] = meta_row_ref[...]
+    for h in range(OWN_HEADS):
+        key_rich[h] = nt(rich_k_ref[h], keys[h])
+
+    def block(b, carry):
+        start = pl.multiple_of(b * TOK, TOK)
+        rows = pl.ds(start, TOK)
+        window = pl.ds(start, WIN)
+        terms = pair_terms(meta_col_ref[rows], meta_pad[:, window])
+        q_spot = lax.broadcasted_iota(jnp.int32, (TOK, WIN), 0)
+        k_spot = lax.broadcasted_iota(jnp.int32, (TOK, WIN), 1)
+        ahead = k_spot - q_spot
+        place = k_spot + (start - RADIUS)
+        mask = (ahead >= 0) & (ahead <= 2 * RADIUS) & (place >= 0) & (place < ROWS)
+        for h in range(OWN_HEADS):
+            query = qkv_ref[h, rows]
+            query_rich = nn(query, rich_q_ref[h])
+            right = key_rich[h, :, window]
+            scores = nt(query, keys[h, window]) * SCORE_SCALE
+            spread = None
+            for c, (before, distance) in enumerate(terms):
+                logit = query_rich[:, c : c + 1] + right[c : c + 1]
+                logit = jnp.where(before, logit, -logit)
+                off = distance - (query_rich[:, 2 + c : 3 + c] + right[2 + c : 3 + c])
+                scores = scores + (jnp.minimum(logit, 0.0) - 0.5 * off * off)
+                grown = 1.0 + jnp.exp(-jnp.abs(logit))
+                spread = grown if spread is None else spread * grown
+            scores = jnp.where(mask, scores - jnp.log(spread), MASKED)
+            glob_scores = nt(query, qkv_ref[OWN_HEADS + h, ROWS:]) * SCORE_SCALE
+            top = jnp.maximum(
+                jnp.max(scores, axis=-1, keepdims=True), jnp.max(glob_scores, axis=-1, keepdims=True)
+            )
+            prob = jnp.exp(scores - top)
+            glob_prob = jnp.exp(glob_scores - top)
+            total = jnp.sum(prob, axis=-1, keepdims=True) + jnp.sum(
+                glob_prob, axis=-1, keepdims=True
+            )
+            inverse = 1.0 / total
+            prob = prob * inverse
+            glob_prob = glob_prob * inverse
+            prob_ref[h, rows] = prob
+            glob_prob_ref[h, rows] = glob_prob
+            mixed = nn(prob.astype(BF), values[h, window]) + nn(
+                glob_prob.astype(BF), qkv_ref[2 * OWN_HEADS + h, ROWS:]
+            )
+            attn_ref[rows, h * HEAD_DIM : (h + 1) * HEAD_DIM] = mixed.astype(BF)
+        return carry
+
+    lax.fori_loop(0, SEQ_WAYS, block, 0)
+    slot = lax.broadcasted_iota(jnp.int32, (GLOBALS, ROWS), 0).astype(F32)
+    member = meta_row_ref[10:11] == slot
+    for h in range(OWN_HEADS):
+        query = qkv_ref[h, ROWS:]
+        scores = nt(query, qkv_ref[OWN_HEADS + h, :ROWS]) * SCORE_SCALE
+        scores = jnp.where(member, scores, MASKED)
+        own = nt(query, qkv_ref[OWN_HEADS + h, ROWS:]) * SCORE_SCALE
+        top = jnp.maximum(
+            jnp.max(scores, axis=-1, keepdims=True), jnp.max(own, axis=-1, keepdims=True)
+        )
+        prob = jnp.exp(scores - top)
+        own_prob = jnp.exp(own - top)
+        total = jnp.sum(prob, axis=-1, keepdims=True) + jnp.sum(own_prob, axis=-1, keepdims=True)
+        inverse = 1.0 / total
+        prob = prob * inverse
+        own_prob = own_prob * inverse
+        member_ref[h] = prob
+        self_ref[h] = own_prob
+        mixed = nn(prob.astype(BF), qkv_ref[2 * OWN_HEADS + h, :ROWS]) + nn(
+            own_prob.astype(BF), qkv_ref[2 * OWN_HEADS + h, ROWS:]
+        )
+        glob_att_ref[h] = mixed
+        attn_ref[ROWS:, h * HEAD_DIM : (h + 1) * HEAD_DIM] = mixed.astype(BF)
+
+
+def feed_kernel(
+    me_ref, att_a, att_b, att_c, att_d, cot_a, cot_b, cot_c, cot_d, cot_glob_ref, super_ref,
+    glob_ref, w_out_ref, w_up_ref, w_down_ref, bias_ref, gain_ref, shift_ref,
+    y_ref, normed_ref, hidden_ref, d_pre_ref, cot_ref, out_ref, back_ref, d_bias_ref, cot_sum_ref,
+):
+    me = me_ref[0]
+    for k, cot in enumerate((cot_a, cot_b, cot_c, cot_d)):
+        cot_ref[pl.ds(pl.multiple_of((me ^ k) * TOK, TOK), TOK)] = cot[...]
+    cot_ref[ROWS:] = cot_glob_ref[...]
+    gain, shift, bias = gain_ref[...], shift_ref[...], bias_ref[...]
+    d_bias = jnp.zeros((1, FF_OWN), F32)
+    cot_sum = jnp.zeros((1, D), F32)
+    tile = 192
+    for low in range(0, ALL, tile):
+        rows = slice(low, low + tile)
+        if low + tile <= ROWS:
+            y_rows = super_ref[rows]
+        else:
+            y_rows = jnp.concatenate([super_ref[low:], glob_ref[...].astype(F32)], axis=0)
+        for k, att in enumerate((att_a, att_b, att_c, att_d)):
+            y_rows = y_rows + nn(att[rows], w_out_ref[pl.ds(pl.multiple_of((me ^ k) * OWN, OWN), OWN)])
+        y_ref[rows] = y_rows
+        normed = (row_stats(y_rows)[0] * gain + shift).astype(BF)
+        normed_ref[rows] = normed
+        hidden, slope = gelu_parts(nn(normed, w_up_ref[...]) + bias)
+        hidden = hidden.astype(BF)
+        hidden_ref[rows] = hidden
+        cot = cot_ref[rows]
+        cot_sum = cot_sum + jnp.sum(cot.astype(F32), axis=0, keepdims=True)
+        d_pre = (nt(cot, w_down_ref[...]) * slope).astype(BF)
+        d_pre_ref[rows] = d_pre
+        d_bias = d_bias + jnp.sum(d_pre.astype(F32), axis=0, keepdims=True)
+        out_part = nn(hidden, w_down_ref[...]).astype(BF)
+        back_part = nt(d_pre, w_up_ref[...]).astype(BF)
+        for ref, part in ((out_ref, out_part), (back_ref, back_part)):
+            spot = low
+            while spot < low + tile:
+                if spot < ROWS:
+                    b, inner = spot // TOK, spot % TOK
+                    count = min(TOK - inner, low + tile - spot)
+                    ref[b, inner : inner + count] = part[spot - low : spot - low + count]
+                else:
+                    b, count = (spot - ROWS) // GLOB_OWN, GLOB_OWN
+                    ref[b, TOK:] = part[spot - low : spot - low + count]
+                spot = spot + count
+    d_bias_ref[...] = d_bias
+    cot_sum_ref[...] = cot_sum
+
+
+def back_kernel(
+    me_ref, back_a, back_b, back_c, back_d, y_ref, cot_ref, w_out_ref, gain_ref,
+    qkv_ref, meta_col_ref, meta_row_ref, rich_q_ref, rich_k_ref, prob_ref, glob_prob_ref,
+    member_ref, self_ref, glob_att_ref, rich_qt_ref, rich_kt_ref,
+    d_y_ref, d_proj_ref, d_qkv_ref, vec_ref, grad_rich_ref,
+    keys, values, key_rich, meta_pad, d_norm, d_att, d_keys, d_values, d_key_rich, d_query_rich,
+):
+    me = me_ref[0]
+    for k, back in enumerate((back_a, back_b, back_c, back_d)):
+        at = me ^ k
+        d_norm[pl.ds(pl.multiple_of(at * TOK, TOK), TOK)] = back[:TOK]
+        d_norm[pl.ds(pl.multiple_of(ROWS + at * GLOB_OWN, GLOB_OWN), GLOB_OWN)] = back[TOK:]
+    gain = gain_ref[...]
+    d_gain = jnp.zeros((1, D), F32)
+    d_shift = jnp.zeros((1, D), F32)
+    for low in range(0, ALL, 192):
+        rows = slice(low, low + 192)
+        d_rows, gain_part, shift_part = norm_back(d_norm[rows].astype(F32), gain, y_ref[rows])
+        d_rows = cot_ref[rows].astype(F32) + d_rows
+        d_y_ref[rows] = d_rows
+        d_proj = d_rows.astype(BF)
+        d_proj_ref[rows] = d_proj
+        d_gain = d_gain + gain_part
+        d_shift = d_shift + shift_part
+        projected = nt(d_proj, w_out_ref[...]).astype(BF)
+        for h in range(OWN_HEADS):
+            d_att[h, rows] = projected[:, h * HEAD_DIM : (h + 1) * HEAD_DIM]
+    vec_ref[...] = jnp.zeros((8, D), F32)
+    vec_ref[0:1] = d_gain
+    vec_ref[1:2] = d_shift
+
+    edge = jnp.zeros((OWN_HEADS, RADIUS, HEAD_DIM), BF)
+    for held, first in ((keys, OWN_HEADS), (values, 2 * OWN_HEADS)):
+        held[:, :RADIUS] = edge
+        held[:, RADIUS + ROWS :] = edge
+        held[:, RADIUS : RADIUS + ROWS] = qkv_ref[first : first + OWN_HEADS, :ROWS]
+    meta_pad[...] = jnp.zeros((16, PAD), F32)
+    meta_pad[:, RADIUS : RADIUS + ROWS] = meta_row_ref[...]
+    for h in range(OWN_HEADS):
+        key_rich[h] = nt(rich_k_ref[h], keys[h])
+    d_keys[...] = jnp.zeros((OWN_HEADS, PAD, HEAD_DIM), F32)
+    d_values[...] = jnp.zeros((OWN_HEADS, PAD, HEAD_DIM), F32)
+    d_key_rich[...] = jnp.zeros((OWN_HEADS, 8, PAD), F32)
+    glob_key = [qkv_ref[OWN_HEADS + h, ROWS:] for h in range(OWN_HEADS)]
+    glob_value = [qkv_ref[2 * OWN_HEADS + h, ROWS:] for h in range(OWN_HEADS)]
+
+    def block(b, carry):
+        start = pl.multiple_of(b * TOK, TOK)
+        rows = pl.ds(start, TOK)
+        window = pl.ds(start, WIN)
+        terms = pair_terms(meta_col_ref[rows], meta_pad[:, window])
+        carry = list(carry)
+        for h in range(OWN_HEADS):
+            query = qkv_ref[h, rows]
+            d_out = d_att[h, rows]
+            prob = prob_ref[h, rows]
+            glob_prob = glob_prob_ref[h, rows]
+            d_prob = nt(d_out, values[h, window])
+            d_glob_prob = nt(d_out, glob_value[h])
+            delta = jnp.sum(prob * d_prob, axis=-1, keepdims=True) + jnp.sum(
+                glob_prob * d_glob_prob, axis=-1, keepdims=True
+            )
+            d_scores = prob * (d_prob - delta)
+            d_low = d_scores.astype(BF)
+            d_glob_low = (glob_prob * (d_glob_prob - delta)).astype(BF)
+            query_rich = nn(query, rich_q_ref[h])
+            right = key_rich[h, :, window]
+            lefts = []
+            for c, (before, distance) in enumerate(terms):
+                logit = query_rich[:, c : c + 1] + right[c : c + 1]
+                pulled = jnp.where(before, 0.5, -0.5) - 0.5 * jnp.tanh(0.5 * logit)
+                pulled = d_scores * pulled
+                off = distance - (query_rich[:, 2 + c : 3 + c] + right[2 + c : 3 + c])
+                off = d_scores * off
+                lefts.append((c, jnp.sum(pulled, axis=-1, keepdims=True)))
+                lefts.append((2 + c, jnp.sum(off, axis=-1, keepdims=True)))
+                d_key_rich[h, c : c + 1, window] += jnp.sum(pulled, axis=0, keepdims=True)
+                d_key_rich[h, 2 + c : 3 + c, window] += jnp.sum(off, axis=0, keepdims=True)
+            lane = lax.broadcasted_iota(jnp.int32, (TOK, 8), 1)
+            d_left = jnp.zeros((TOK, 8), F32)
+            d_query = (nn(d_low, keys[h, window]) + nn(d_glob_low, glob_key[h])) * SCORE_SCALE
+            for c, column in lefts:
+                d_left = jnp.where(lane == c, column, d_left)
+                d_query = d_query + column * rich_qt_ref[h, c : c + 1]
+            d_query_rich[h, rows] = d_left
+            d_qkv_ref[rows, h * HEAD_DIM : (h + 1) * HEAD_DIM] = d_query.astype(BF)
+            d_keys[h, window] += tn(d_low, query) * SCORE_SCALE
+            d_values[h, window] += tn(prob.astype(BF), d_out)
+            carry[2 * h] = carry[2 * h] + tn(d_glob_low, query) * SCORE_SCALE
+            carry[2 * h + 1] = carry[2 * h + 1] + tn(glob_prob.astype(BF), d_out)
+        return tuple(carry)
+
+    zero = jnp.zeros((GLOBALS, HEAD_DIM), F32)
+    sums = lax.fori_loop(0, SEQ_WAYS, block, (zero,) * (2 * OWN_HEADS))
+    for h in range(OWN_HEADS):
+        span = slice(h * HEAD_DIM, (h + 1) * HEAD_DIM)
+        key_span = slice(OWN + h * HEAD_DIM, OWN + (h + 1) * HEAD_DIM)
+        value_span = slice(2 * OWN + h * HEAD_DIM, 2 * OWN + (h + 1) * HEAD_DIM)
+        query = qkv_ref[h, ROWS:]
+        key_rows = qkv_ref[OWN_HEADS + h, :ROWS]
+        value_rows = qkv_ref[2 * OWN_HEADS + h, :ROWS]
+        d_out = d_att[h, ROWS:]
+        delta = jnp.sum(d_out.astype(F32) * glob_att_ref[h], axis=-1, keepdims=True)
+        prob, own_prob = member_ref[h], self_ref[h]
+        d_low = (prob * (nt(d_out, value_rows) - delta)).astype(BF)
+        d_own = (own_prob * (nt(d_out, glob_value[h]) - delta)).astype(BF)
+        d_query = (nn(d_low, key_rows) + nn(d_own, glob_key[h])) * SCORE_SCALE
+        d_qkv_ref[ROWS:, span] = d_query.astype(BF)
+        d_qkv_ref[ROWS:, key_span] = (sums[2 * h] + tn(d_own, query) * SCORE_SCALE).astype(BF)
+        d_qkv_ref[ROWS:, value_span] = (sums[2 * h + 1] + tn(own_prob.astype(BF), d_out)).astype(BF)
+        d_right = d_key_rich[h, :, RADIUS : RADIUS + ROWS]
+        d_key = d_keys[h, RADIUS : RADIUS + ROWS] + tn(d_low, query) * SCORE_SCALE
+        d_key = d_key + lax.dot_general(
+            d_right, rich_kt_ref[h], (((0,), (0,)), ((), ())), precision=PRECISE,
+            preferred_element_type=F32,
+        )
+        d_value = d_values[h, RADIUS : RADIUS + ROWS] + tn(prob.astype(BF), d_out)
+        d_qkv_ref[:ROWS, key_span] = d_key.astype(BF)
+        d_qkv_ref[:ROWS, value_span] = d_value.astype(BF)
+        grad_rich_ref[h] = tn(d_query_rich[h].astype(BF), qkv_ref[h, :ROWS])
+        grad_rich_ref[OWN_HEADS + h] = nn(d_right.astype(BF), key_rows)
+
+
+def last_kernel(
+    me_ref, dqkv_a, dqkv_b, dqkv_c, dqkv_d, w_qkv_ref, super_ref, glob_ref, d_y_ref, pre_ref,
+    w_graph_ref, meta_col_ref, gain_ref,
+    grad_tok_ref, grad_glob_ref, d_pre_ref, vec_ref, d_super,
+):
+    me = me_ref[0]
+    gain = gain_ref[...]
+    d_gain = jnp.zeros((1, D), F32)
+    d_shift = jnp.zeros((1, D), F32)
+    for low in range(0, ALL, 192):
+        rows = slice(low, low + 192)
+        inner = min(192, ROWS - low)
+        d_norm = None
+        for k, part in enumerate((dqkv_a, dqkv_b, dqkv_c, dqkv_d)):
+            term = nt(part[rows], w_qkv_ref[me ^ k])
+            d_norm = term if d_norm is None else d_norm + term
+        if inner == 192:
+            rows_in = super_ref[rows]
+        else:
+            rows_in = jnp.concatenate([super_ref[low:], glob_ref[...].astype(F32)], axis=0)
+        back, gain_part, shift_part = norm_back(d_norm, gain, rows_in)
+        d_gain = d_gain + gain_part
+        d_shift = d_shift + shift_part
+        back = back + d_y_ref[rows]
+        d_super[rows] = back
+        long = slice(low, low + inner)
+        slope = gelu_parts(pre_ref[long])[1]
+        d_pre_ref[long] = (back[:inner] * slope).astype(BF)
+    grad_glob_ref[...] = d_super[ROWS:]
+    vec_ref[...] = jnp.zeros((8, D), F32)
+    vec_ref[0:1] = d_gain
+    vec_ref[1:2] = d_shift
+    total = d_super[pl.ds(pl.multiple_of(me * TOK, TOK), TOK)]
+    for shift in (-1, 0, 1):
+        b = me - shift
+        fits = (b >= 0) & (b < SEQ_WAYS)
+        rows = pl.ds(pl.multiple_of(jnp.clip(b, 0, SEQ_WAYS - 1) * TOK, TOK), TOK)
+        d_agg = (nt(d_pre_ref[rows], w_graph_ref[...]) * (1.0 / NEIGH)).astype(BF)
+        neigh = meta_col_ref[rows].astype(jnp.int32)
+        counts = counts_of(neigh, (shift + 1) * TOK, TOK)
+        total = total + jnp.where(fits, tn(counts, d_agg), 0.0)
+    grad_tok_ref[...] = total
+
+
+def call(kernel, ins, outs, scratch=(), flops=0, moved=0, scalars=1):
+    specs = [pl.BlockSpec(memory_space=pltpu.SMEM)] * scalars
+    specs += [pl.BlockSpec(memory_space=pltpu.VMEM)] * (len(ins) - scalars)
+    return pl.pallas_call(
+        kernel,
+        out_shape=[jax.ShapeDtypeStruct(shape, kind) for shape, kind in outs],
+        in_specs=specs,
+        out_specs=[pl.BlockSpec(memory_space=pltpu.VMEM)] * len(outs),
+        scratch_shapes=[pltpu.VMEM(shape, kind) for shape, kind in scratch],
+        compiler_params=pltpu.CompilerParams(vmem_limit_bytes=48 * 1024 * 1024),
+        cost_estimate=pl.CostEstimate(flops=flops, bytes_accessed=moved, transcendentals=0),
+    )(*ins)
+
+
+def split_heads(
+    tokens, global_tokens, neighbours, token_ranks, membership, w_graph, gain_one, shift_one,
+    w_query, w_key, w_value, rich_query, rich_key, w_out, gain_two, shift_two, w_up, bias_up,
+    w_down, bias_down, cot_tokens, cot_global,
+):
+    me = lax.axis_index("seq")
+    me_arr = me.reshape(1).astype(jnp.int32)
+    ints = jnp.concatenate([neighbours, token_ranks.T, membership[:, None]], axis=1)
+    ints = jnp.pad(ints, ((0, 0), (0, 128 - ints.shape[1])))
+    tok_blocks = gather_seq(tokens)
+    int_blocks = gather_seq(ints)
+    cot_blocks = gather_seq(cot_tokens)
+
+    def own_columns(weight, width):
+        return lax.dynamic_slice_in_dim(weight, me * width, width, axis=1)
+
+    def row(vector):
+        return vector.reshape(1, -1)
+
+    w_all = jnp.stack([w.reshape(D, SEQ_WAYS, OWN) for w in (w_query, w_key, w_value)], axis=2)
+    w_all = w_all.transpose(1, 0, 2, 3).reshape(SEQ_WAYS, D, 3 * OWN)
+    w_qkv = pick(w_all, me)
+    w_up_own = own_columns(w_up, FF_OWN)
+    w_down_own = lax.dynamic_slice_in_dim(w_down, me * FF_OWN, FF_OWN, axis=0)
+    w_out_own = lax.dynamic_slice_in_dim(w_out, me * OWN, OWN, axis=0)
+    bias_own = row(lax.dynamic_slice_in_dim(bias_up, me * FF_OWN, FF_OWN, axis=0))
+
+    def own_rich(rich):
+        rich = own_columns(rich, 4 * OWN_HEADS).reshape(HEAD_DIM, OWN_HEADS, 4)
+        return rich.transpose(1, 0, 2)
+
+    rich_q_own, rich_k_own = own_rich(rich_query), own_rich(rich_key)
+    rich_q_in = jnp.pad(rich_q_own, ((0, 0), (0, 0), (0, 124)))
+    rich_kt = jnp.pad(rich_k_own.transpose(0, 2, 1), ((0, 0), (0, 4), (0, 0)))
+    rich_qt = jnp.pad(rich_q_own.transpose(0, 2, 1), ((0, 0), (0, 4), (0, 0)))
+
+    agg, graph_pre, super_rows, normed, qkv, meta_col, meta_row = call(
+        graph_kernel,
+        [me_arr, *tok_blocks, *int_blocks, global_tokens, w_graph, w_qkv, row(gain_one), row(shift_one)],
+        [((ROWS, D), BF), ((ROWS, D), F32), ((ROWS, D), F32), ((ALL, D), BF),
+         ((3 * OWN_HEADS, ALL, HEAD_DIM), BF), ((ROWS, 128), F32), ((16, ROWS), F32)],
+        [((PAD, D), BF)],
+        flops=1_500_000_000, moved=9_000_000,
+    )
+    heads_scratch = [
+        ((OWN_HEADS, PAD, HEAD_DIM), BF), ((OWN_HEADS, PAD, HEAD_DIM), BF),
+        ((OWN_HEADS, 8, PAD), F32), ((16, PAD), F32),
+    ]
+    attn, prob, glob_prob, member_prob, self_prob, glob_att = call(
+        attend_kernel,
+        [qkv, meta_col, meta_row, rich_q_in, rich_kt],
+        [((ALL, OWN), BF), ((OWN_HEADS, ROWS, WIN), F32), ((OWN_HEADS, ROWS, GLOBALS), F32),
+         ((OWN_HEADS, GLOBALS, ROWS), F32), ((OWN_HEADS, GLOBALS, GLOBALS), F32),
+         ((OWN_HEADS, GLOBALS, HEAD_DIM), F32)],
+        heads_scratch,
+        flops=4_000_000_000, moved=6_000_000, scalars=0,
+    )
+    att_blocks = gather_seq(attn)
+    y_rows, normed_two, hidden, d_pre, cot_all, out_parts, back_parts, d_bias_up, cot_sum = call(
+        feed_kernel,
+        [me_arr, *att_blocks, *cot_blocks, cot_global, super_rows, global_tokens, w_out, w_up_own,
+         w_down_own, bias_own, row(gain_two), row(shift_two)],
+        [((ALL, D), F32), ((ALL, D), BF), ((ALL, FF_OWN), BF), ((ALL, FF_OWN), BF), ((ALL, D), BF),
+         ((SEQ_WAYS, CHUNK, D), BF), ((SEQ_WAYS, CHUNK, D), BF), ((1, FF_OWN), F32), ((1, D), F32)],
+        flops=4_000_000_000, moved=12_000_000,
+    )
+    back_blocks = gather_seq(scatter_seq(back_parts).astype(BF))
+    grad_down = tn(hidden, cot_all).astype(BF).reshape(GRP_WAYS, FF_OWN // GRP_WAYS, D)
+    grad_up = rows_to_chunks(tn(normed_two, d_pre).astype(BF))
+    down_sum = gather_grp(reduce_grp(grad_down))
+    up_sum = gather_grp(turned_reduce(grad_up))
+    out_own = scatter_seq(out_parts)
+    own_start = me * TOK
+    glob_start = ROWS + me * GLOB_OWN
+    out_tokens = (
+        lax.dynamic_slice_in_dim(y_rows, own_start, TOK, 0) + out_own[:TOK] + bias_down
+    ).astype(BF)
+    out_glob = (
+        lax.dynamic_slice_in_dim(y_rows, glob_start, GLOB_OWN, 0) + out_own[TOK:] + bias_down
+    ).astype(BF)
+    out_global = jnp.stack(gather_seq(out_glob))[jnp.arange(SEQ_WAYS) ^ me].reshape(GLOBALS, D)
+
+    d_y, d_proj, d_qkv, vec_two, grad_rich = call(
+        back_kernel,
+        [me_arr, *back_blocks, y_rows, cot_all, w_out_own, row(gain_two), qkv, meta_col, meta_row,
+         rich_q_in, rich_kt, prob, glob_prob, member_prob, self_prob, glob_att,
+         rich_qt.astype(F32), rich_kt.astype(F32)],
+        [((ALL, D), F32), ((ALL, D), BF), ((ALL, 3 * OWN), BF), ((8, D), F32),
+         ((2 * OWN_HEADS, 8, HEAD_DIM), F32)],
+        heads_scratch + [
+            ((ALL, D), BF), ((OWN_HEADS, ALL, HEAD_DIM), BF), ((OWN_HEADS, PAD, HEAD_DIM), F32),
+            ((OWN_HEADS, PAD, HEAD_DIM), F32), ((OWN_HEADS, 8, PAD), F32),
+            ((OWN_HEADS, ROWS, 8), F32),
+        ],
+        flops=6_000_000_000, moved=14_000_000,
+    )
+    d_qkv_blocks = gather_seq(d_qkv)
+    grad_qkv = rows_to_chunks(tn(normed, d_qkv).astype(BF))
+    qkv_sum = gather_grp(turned_reduce(grad_qkv))
+    grad_out = tn(attn, d_proj)
+    own_bits = [
+        lax.dynamic_slice_in_dim(vector, me * OWN, OWN, 0)
+        for vector in (vec_two[0], vec_two[1], cot_sum[0])
+    ]
+    small = jnp.concatenate([*own_bits, d_bias_up[0], grad_rich[:, :4].reshape(-1)])
+    out_sum = gather_grp(reduce_grp(with_small(grad_out, small)))
+
+    grad_tokens, grad_global, d_graph_pre, vec_one = call(
+        last_kernel,
+        [me_arr, *d_qkv_blocks, w_all, super_rows, global_tokens, d_y, graph_pre, w_graph, meta_col,
+         row(gain_one)],
+        [((TOK, D), F32), ((GLOBALS, D), F32), ((ROWS, D), BF), ((8, D), F32)],
+        [((ALL, D), F32)],
+        flops=4_000_000_000, moved=12_000_000,
+    )
+    grad_graph = tn(own_columns(agg, OWN), d_graph_pre)
+    small_last = jnp.concatenate(
+        [lax.dynamic_slice_in_dim(vector, me * OWN, OWN, 0) for vector in (vec_one[0], vec_one[1])]
+    )
+    graph_sum = gather_grp(reduce_grp(with_small(grad_graph, small_last)))
+
+    g_down = down_sum.astype(F32).reshape(FF_OWN, D)
+    g_up = chunks_to_rows(up_sum, FF_OWN)
+    g_qkv = chunks_to_rows(qkv_sum, 3 * OWN).reshape(OWN, SEQ_WAYS, 3, OWN)
+    g_query, g_key, g_value = (g_qkv[:, :, i].reshape(OWN, D) for i in range(3))
+    g_out = out_sum[:, :24].astype(F32).reshape(OWN, D)
+    g_graph = graph_sum[:, :24].astype(F32).reshape(OWN, D)
+    bits = out_sum[0, 24:].astype(F32).reshape(-1)
+    last_bits = graph_sum[0, 24:].astype(F32).reshape(-1)
+    g_gain_two, g_shift_two, g_bias_down = (bits[i * OWN : (i + 1) * OWN] for i in range(3))
+    g_bias_up = bits[3 * OWN : 3 * OWN + FF_OWN]
+    rich = bits[3 * OWN + FF_OWN :][: 2 * OWN_HEADS * 4 * HEAD_DIM]
+    rich = rich.reshape(8, -1).astype(BF)
+    rich = jnp.stack(gather_seq(rich))[jnp.arange(SEQ_WAYS) ^ me]
+    rich = rich.reshape(SEQ_WAYS, 2, OWN_HEADS, 4, HEAD_DIM).transpose(1, 4, 0, 2, 3)
+    rich = rich.reshape(2, HEAD_DIM, 4 * HEADS).astype(F32)
+    rich = lax.dynamic_slice_in_dim(rich, me * (HEAD_DIM // SEQ_WAYS), HEAD_DIM // SEQ_WAYS, 1)
+    return (
+        out_tokens, out_global, grad_tokens, grad_global,
+        g_graph, last_bits[:OWN], last_bits[OWN : 2 * OWN], g_query, g_key, g_value, rich[0], rich[1],
+        g_out, g_gain_two, g_shift_two, g_up, g_bias_up, g_down, g_bias_down,
+    )
+
+
+def rows_to_chunks(grad):
+    part = D // SEQ_WAYS // GRP_WAYS
+    grad = grad.reshape(SEQ_WAYS, GRP_WAYS, part, grad.shape[1]).transpose(1, 0, 2, 3)
+    return grad.reshape(GRP_WAYS, SEQ_WAYS * part, grad.shape[3])
+
+
+def turned_reduce(chunks):
+    mine = reduce_grp(chunks).astype(BF)
+    part = D // SEQ_WAYS // GRP_WAYS
+    return turn_seq(mine.reshape(SEQ_WAYS, part, mine.shape[1])).reshape(mine.shape)
+
+
+def chunks_to_rows(chunks, width):
+    part = D // SEQ_WAYS // GRP_WAYS
+    chunks = chunks.reshape(GRP_WAYS, SEQ_WAYS, part, width).transpose(0, 2, 1, 3)
+    return chunks.reshape(GRP_WAYS * part, SEQ_WAYS * width).astype(F32)
+
+
+def with_small(grad, small):
+    part = D // SEQ_WAYS // GRP_WAYS
+    grad = grad.astype(BF).reshape(GRP_WAYS, part, D)
+    small = jnp.pad(small.astype(BF), (0, 8 * D - small.shape[0])).reshape(1, 8, D)
+    return jnp.concatenate([grad, jnp.broadcast_to(small, (GRP_WAYS, 8, D))], axis=1)
+
+
+def layer(*arrays):
+    tokens, global_tokens = arrays[:2]
+    ways = (lax.axis_size("seq"), lax.axis_size("grp"))
+    if ways == (SEQ_WAYS, GRP_WAYS) and tokens.shape[0] == TOK and global_tokens.shape[0] == GLOBALS:
+        return split_heads(*arrays)
+    return local(*arrays)
+
+
 def solution(mesh):
     return jax.shard_map(
-        local,
+        layer,
         mesh=mesh,
         in_specs=(
             P(("grp", "seq"), None),

time: 1260 us -> 317 us (0.25)
  other arithmetic: 324 us -> 26.7 us
  local copies, waits for them, and re-layouts: 311 us -> 64.4 us
  blocking collectives: 201 us -> 0 us
  waiting for transfers between devices: 244 us -> 89.6 us
  matrix products: 122 us -> 4.98 us
  Pallas kernels: 0 us -> 63.8 us
  starting transfers between devices: 29.4 us -> 62.9 us
  between operations: 18.2 us -> 2.31 us
    unnamed x492 -> x99, local copies, waits for them, and re-layouts: 220 us -> 20 us
    all_to_all x1 -> x0, blocking collectives: 178 us -> none  [local(): lax.all_to_all(packed.astype(jnp.bfloat16), 'seq', split_axis=0, concat_a...]
    unnamed x3 -> x0, waiting for transfers between devices: 125 us -> none
    reduce_sum x21 -> x0, other arithmetic: 118 us -> none  [the longest x1 84.1 us: local(): group_total = jnp.sum(received, axis=0).reshape(group_count, -1)]
    dot_general x69 -> x5, matrix products: 122 us -> 4.98 us  [tn(): lax.dot_general(left, right, (((0,), (0,)), ((), ())), preferred_element_...]
    concatenate x3 -> x4, other arithmetic: 94.7 us -> 0.84 us  [the longest x1 0.73 us: split_heads(): jnp.concatenate([neighbours, token_ranks.T, membership[:, None]], axis=1)]
    ppermute x10 -> x62, waiting for transfers between devices: 0.03 us -> 89.6 us  [the longest x5 25.8 us: reduce_grp(): lax.ppermute(sent, 'grp', X_SWAP).astype(F32)]
    all_to_all x1 -> x0, waiting for transfers between devices: 84.6 us -> none  [local(): lax.all_to_all(group_total.astype(jnp.bfloat16), 'grp', split_axis=0, con...]
  transfers between devices with their start and end apart: 13 -> 62, of which waited for: 3 -> 23; matrix products, arithmetic and copies ran while one was open for 11% -> 26% of each run, Pallas kernels for 0% -> 17%
where the time goes in v1:
time: 317 us; the launch traced here: 315 us
  waiting for transfers between devices  89.6 us (28%)
  local copies, waits for them, and re-layouts  64.4 us (20%)
  Pallas kernels  63.8 us (20%)
  starting transfers between devices  62.9 us (20%)
  other arithmetic  26.7 us (8%)
  matrix products  4.98 us (2%)
    pallas_call x5, Pallas kernels, call(): pl.pallas_call(kernel, out_shape=[jax.ShapeDtypeStruct(shape, kind) for s...  63.8 us
    ppermute x5, waiting for transfers between devices, reduce_grp(): lax.ppermute(sent, 'grp', X_SWAP).astype(F32)  25.8 us
    ppermute x5, waiting for transfers between devices, reduce_grp(): came = lax.ppermute(pick(part, 1 - z_high), 'grp', Z_FAR)  20.2 us
    unnamed x99, local copies, waits for them, and re-layouts  20 us
    ppermute x5, starting transfers between devices, gather_grp(): held = both(z_low, held, lax.ppermute(held, 'grp', Z_NEAR), 1)  13.8 us
    ppermute x5, waiting for transfers between devices, reduce_grp(): lax.ppermute(sent, 'grp', Z_NEAR).astype(F32)  12.3 us
    ppermute x2, waiting for transfers between devices, turn_seq(): far = lax.ppermute(pick(pair, 1 - y), 'seq', Y_SWAP)  11 us
    ppermute x8, starting transfers between devices, gather_seq(): across = lax.ppermute(block, 'seq', Y_SWAP)  9.97 us
  transfers between devices with their start and end apart: 62, of which 23 were waited for; matrix products, arithmetic and copies ran while one was open for 26% of the time, Pallas kernels for 17%

profile of v1, /device:TPU:0, one launch (start us, length us, event | category | flops | bytes accessed | tf_op | source)
XLA Modules:
  0.0 314.8 jit_solution(17693668935942885647)
XLA Ops:
  1.2 2.6 collective-permute-start.1
  5.2 2.4 copy.133
  7.6 2.4 copy.132
  9.9 2.4 copy.131
  12.3 2.2 maximum_bitcast_fusion
  14.5 2.1 copy.134
  20.1 1.8 collective-permute-start.10
  23.2 5.0 %shard_map.357 = (bf16[512,768]{1,0:T(8,128)(2,1)S(1)}, f32[512,768]{1,0:T(8,128)}, f32[512,768]{1,0:T(8,128)}, bf16[576,768]{1,0:T(8,128)(2,1)S(1)}, bf16[9,576...) custom-call(s32[1]{0:T(128)} %bitcast.me_ref, bf16[128,768]{1,0:T(8,128)(2,1)S(1)} %copy-done.6, ...), custom_call_target="tpu_custom_call" | custom-call | flops 1500000000 | bytes 9000000 | tf_op jit(solution)/shard_map/pallas_call | solution.py:1061
  30.6 10.1 %shard_map.358 = (bf16[576,192]{1,0:T(8,128)(2,1)S(1)}, f32[3,512,384]{2,1,0:T(8,128)S(1)}, f32[3,512,64]{2,1,0:T(8,128)S(1)}, f32[3,64,512]{2,1,0:T(8,128)S(1)}...) custom-call(bf16[9,576,64]{2,1,0:T(8,128)(2,1)S(1)} %copy-done.12, f32[512,128]{1,0:T(8,128)S(1)} %get-tuple-element.51.meta_col_ref, ...), custom_call_target="tpu_custom_call" | custom-call | flops 4000000000 | bytes 6000000 | tf_op jit(solution)/shard_map/pallas_call | solution.py:1061
  45.6 6.4 %collective-permute-done.7.att_c = bf16[576,192]{1,0:T(8,128)(2,1)S(1)} collective-permute-done((bf16[576,192]{1,0:T(8,128)(2,1)S(1)}, bf16[576,192]{1,0:T(8,128)(2,1)S(1)}, u32[]{:S(2)}, u32[]{:S(2)}) %collective-permute-start.7) | collective-permute-done | bytes 221216 | tf_op jit(solution)/shard_map/ppermute | solution.py:611
  52.1 6.2 %copy.140.w_qkv_ref = bf16[4,768,576]{2,1,0:T(8,128)(2,1)} copy(bf16[4,768,576]{1,2,0:T(8,128)(2,1)} %bitcast.329) | data formatting | bytes 7077888 | tf_op jit(solution)/shard_map/reshape | solution.py:1092
  59.3 3.2 %constant_dynamic-slice_fusion.6 = (bf16[768,768]{1,0:T(8,128)(2,1)}, bf16[768,768]{1,0:T(8,128)(2,1)}) fusion(bf16[3072,768]{1,0:T(8,128)(2,1)} %param.40, s32[]{:T(128)S(6)} %select_n.413, bf16[768,3072]{1,0:T(8,128)(2,1)} %param.38), kind=kLoop, calls=%fused_computation.179 | loop fusion | bytes 4718596 | tf_op jit(solution)/shard_map/dynamic_slice | solution.py:1095
  62.6 9.8 %shard_map.359 = (f32[576,768]{1,0:T(8,128)}, bf16[576,768]{1,0:T(8,128)(2,1)S(1)}, bf16[576,768]{1,0:T(8,128)(2,1)S(1)}, bf16[576,768]{1,0:T(8,128)(2,1)S(1)}, ...) custom-call(s32[1]{0:T(128)} %bitcast.me_ref, ...), custom_call_target="tpu_custom_call" | custom-call | flops 4000000000 | bytes 12000000 | tf_op jit(solution)/shard_map/pallas_call | solution.py:1061
  75.9 1.6 collective-permute-start.48
  82.2 9.9 %collective-permute-done.48 = bf16[4,96,768]{2,1,0:T(8,128)(2,1)S(1)} collective-permute-done((bf16[4,96,768]{2,1,0:T(8,128)(2,1)S(1)}, bf16[4,96,768]{2,1,0:T(8,128)(2,1)S(1)}, u32[]{:S(2)}, u32[]{:S(2)}) %collective-permute-start.48) | collective-permute-done | bytes 589856 | tf_op jit(solution)/shard_map/ppermute | solution.py:649
  92.3 1.6 collective-permute-start.49
  93.9 10.2 %collective-permute-done.56 = bf16[4,96,768]{2,1,0:T(8,128)(2,1)S(1)} collective-permute-done((bf16[4,96,768]{2,1,0:T(8,128)(2,1)S(1)}, bf16[4,96,768]{2,1,0:T(8,128)(2,1)S(1)}, u32[]{:S(2)}, u32[]{:S(2)}) %collective-permute-start.56) | collective-permute-done | bytes 589856 | tf_op jit(solution)/shard_map/ppermute | solution.py:649
  105.1 1.6 collective-permute-start.57
  108.7 1.7 fusion.8
  115.6 2.7 collective-permute-start.50
  120.0 8.4 %collective-permute-done.50 = bf16[96,768]{1,0:T(8,128)(2,1)S(1)} collective-permute-done((bf16[96,768]{1,0:T(8,128)(2,1)S(1)}, bf16[96,768]{1,0:T(8,128)(2,1)S(1)}, u32[]{:S(2)}, u32[]{:S(2)}) %collective-permute-start.50) | collective-permute-done | bytes 147488 | tf_op jit(solution)/shard_map/ppermute | solution.py:654
  129.1 2.3 collective-permute-done.58
  134.8 26.6 %shard_map.360 = (f32[576,768]{1,0:T(8,128)}, bf16[576,768]{1,0:T(8,128)(2,1)S(1)}, bf16[576,576]{1,0:T(8,128)(2,1)S(1)}, f32[8,768]{1,0:T(8,128)S(1)}, f32[6,8,64]{2,1,0:T(8,128)S(1)}) custom-call(s32[1]{0:T(128)} %bitcast.me_ref, bf16[144,768]{1,0:T(8,128)(2,1)S(1)} %fusion.6.back_a, bf16[144,768]{1,0:T(8,128)(2,1)S(1)} %copy-done.3, ...), custom_call_target="tpu_custom_call" | custom-call | flops 6000000000 | bytes 14000000 | tf_op jit(solution)/shard_map/pallas_call | solution.py:1061
  162.4 1.8 convolution_convert_fusion.2
  164.2 2.2 copy.142
  173.1 8.8 %collective-permute-done.52 = bf16[2,24,768]{2,1,0:T(8,128)(2,1)S(1)} collective-permute-done((bf16[2,24,768]{2,1,0:T(8,128)(2,1)S(1)}, bf16[2,24,768]{2,1,0:T(8,128)(2,1)S(1)}, u32[]{:S(2)}, u32[]{:S(2)}) %collective-permute-start.52) | collective-permute-done | bytes 73760 | tf_op jit(solution)/shard_map/ppermute | solution.py:638
  183.5 3.0 collective-permute-start.53
  188.6 3.2 %collective-permute-start.60 = (bf16[2,96,768]{2,1,0:T(8,128)(2,1)S(1)}, bf16[2,96,768]{2,1,0:T(8,128)(2,1)S(1)}, u32[]{:S(2)}, u32[]{:S(2)}) collective-permute-start(bf16[2,96,768]{2,1,0:T(8,128)(2,1)S(1)} %pad_maximum_fusion.8), channel_id=1, source_target_pairs={{0,8},{4,12},{8,0},{12,4},{16,24},{20,28},{24,16},{28,20},{1,9},{5... | collective-permute-start | bytes 884744 | tf_op jit(solution)/shard_map/ppermute | solution.py:669
  193.4 7.4 %collective-permute-done.40 = bf16[2,32,768]{2,1,0:T(8,128)(2,1)S(1)} collective-permute-done((bf16[2,32,768]{2,1,0:T(8,128)(2,1)S(1)}, bf16[2,32,768]{2,1,0:T(8,128)(2,1)S(1)}, u32[]{:S(2)}, u32[]{:S(2)}) %collective-permute-start.40) | collective-permute-done | bytes 98336 | tf_op jit(solution)/shard_map/ppermute | solution.py:653
  201.6 4.7 %collective-permute-done.41 = bf16[32,768]{1,0:T(8,128)(2,1)S(1)} collective-permute-done((bf16[32,768]{1,0:T(8,128)(2,1)S(1)}, bf16[32,768]{1,0:T(8,128)(2,1)S(1)}, u32[]{:S(2)}, u32[]{:S(2)}) %collective-permute-start.41) | collective-permute-done | bytes 49184 | tf_op jit(solution)/shard_map/ppermute | solution.py:654
  207.0 2.1 collective-permute-start.42
  210.0 2.2 collective-permute-done.42
  212.2 2.0 collective-permute-start.61
  214.3 4.6 %collective-permute-start.43 = (bf16[2,32,768]{2,1,0:T(8,128)(2,1)S(1)}, bf16[2,32,768]{2,1,0:T(8,128)(2,1)S(1)}, u32[]{:S(2)}, u32[]{:S(2)}) collective-permute-start(bf16[2,32,768]{2,1,0:T(8,128)(2,1)S(1)} %pad_maximum_fusion.16), channel_id=1, source_target_pairs={{0,8},{4,12},{8,0},{12,4},{16,24},{20,28},{24,16},{28,20},{1,9},{5... | collective-permute-start | bytes 294920 | tf_op jit(solution)/shard_map/ppermute | solution.py:669
  221.4 2.0 collective-permute-start.32
  224.6 3.5 %collective-permute-done.32 = bf16[2,96,576]{2,1,0:T(8,128)(2,1)S(1)} collective-permute-done((bf16[2,96,576]{2,1,0:T(8,128)(2,1)S(1)}, bf16[2,96,576]{2,1,0:T(8,128)(2,1)S(1)}, u32[]{:S(2)}, u32[]{:S(2)}) %collective-permute-start.32) | collective-permute-done | bytes 221216 | tf_op jit(solution)/shard_map/ppermute | solution.py:653
  243.0 2.2 collective-permute-done.35
  246.1 3.0 collective-permute-start.36
  250.4 1.6 copy.163
  252.7 5.4 %collective-permute-start.37 = (bf16[2,96,576]{2,1,0:T(8,128)(2,1)}, bf16[2,96,576]{2,1,0:T(8,128)(2,1)}, u32[]{:S(2)}, u32[]{:S(2)}) collective-permute-start(bf16[2,96,576]{2,1,0:T(8,128)(2,1)} %pad_maximum_fusion.9), channel_id=1, source_target_pairs={{0,8},{4,12},{8,0},{12,4},{16,24},{20,28},{24,16},{28,20},{1,9},{5... | collective-permute-start | bytes 663560 | tf_op jit(solution)/shard_map/ppermute | solution.py:669
  261.0 12.3 %shard_map.361 = (f32[128,768]{1,0:T(8,128)}, f32[64,768]{1,0:T(8,128)}, bf16[512,768]{1,0:T(8,128)(2,1)S(1)}, f32[8,768]{1,0:T(8,128)S(1)}) custom-call(s32[1]{0:T(128)} %bitcast.me_ref, bf16[576,576]{1,0:T(8,128)(2,1)S(1)} %get-tuple-element.64.dqkv_a, bf16[576,576]{1,0:T(8,128)(2,1)} %collective-permute-done.22.dqkv_b, ...), custom_call_target="tpu_custom_call" | custom-call | flops 4000000000 | bytes 12000000 | tf_op jit(solution)/shard_map/pallas_call | solution.py:1061
  275.9 1.6 collective-permute-start.38
  277.5 4.6 %collective-permute-done.25 = bf16[4,32,768]{2,1,0:T(8,128)(2,1)S(1)} collective-permute-done((bf16[4,32,768]{2,1,0:T(8,128)(2,1)S(1)}, bf16[4,32,768]{2,1,0:T(8,128)(2,1)S(1)}, u32[]{:S(2)}, u32[]{:S(2)}) %collective-permute-start.25) | collective-permute-done | bytes 196640 | tf_op jit(solution)/shard_map/ppermute | solution.py:649
  283.7 1.8 copy.174
  289.7 3.8 %collective-permute-done.27 = bf16[32,768]{1,0:T(8,128)(2,1)S(1)} collective-permute-done((bf16[32,768]{1,0:T(8,128)(2,1)S(1)}, bf16[32,768]{1,0:T(8,128)(2,1)S(1)}, u32[]{:S(2)}, u32[]{:S(2)}) %collective-permute-start.27) | collective-permute-done | bytes 49184 | tf_op jit(solution)/shard_map/ppermute | solution.py:654
  293.7 4.8 %collective-permute-done.28 = bf16[32,768]{1,0:T(8,128)(2,1)S(1)} collective-permute-done((bf16[32,768]{1,0:T(8,128)(2,1)S(1)}, bf16[32,768]{1,0:T(8,128)(2,1)S(1)}, u32[]{:S(2)}, u32[]{:S(2)}) %collective-permute-start.28) | collective-permute-done | bytes 49184 | tf_op jit(solution)/shard_map/ppermute | solution.py:668
  300.2 3.3 %reshape.277 = f32[192,4,3,192]{3,2,0,1:T(4,128)S(1)} reshape(f32[8,24,4,576]{3,1,0,2:T(8,128)} %copy.147) | data formatting | bytes 3538944 | tf_op jit(solution)/shard_map/convert_element_type | solution.py:1231
  304.0 2.5 fusion.58
  (344 shorter events, 94.8 us)
Async XLA Ops:
  0.7 21.3 %collective-permute-start = (bf16[128,768]{1,0:T(8,128)(2,1)}, bf16[128,768]{1,0:T(8,128)(2,1)S(1)}, u32[]{:S(2)}, u32[]{:S(2)}) collective-permute-start(bf16[128,768]{1,0:T(8,128)(2,1)} %tok_a.1), channel_id=1, source_target_pairs={{0,1},{1,0},{2,3},{3,2},{4,5},{5,4},{6,7},{7,6},{8,9},{9,8},{10,11... | collective-permute-start | bytes 589832 | tf_op jit(solution)/shard_map/ppermute | solution.py:612
  1.2 18.3 %collective-permute-start.1 = (bf16[128,768]{1,0:T(8,128)(2,1)}, bf16[128,768]{1,0:T(8,128)(2,1)S(1)}, u32[]{:S(2)}, u32[]{:S(2)}) collective-permute-start(bf16[128,768]{1,0:T(8,128)(2,1)} %tok_a.1), channel_id=1, source_target_pairs={{0,2},{2,0},{1,3},{3,1},{4,6},{6,4},{5,7},{7,5},{8,10},{10,8},{9,1... | collective-permute-start | bytes 589832 | tf_op jit(solution)/shard_map/ppermute | solution.py:611
  4.6 15.5 %collective-permute-start.3 = (s32[128,128]{1,0:T(8,128)S(1)}, s32[128,128]{1,0:T(8,128)S(1)}, u32[]{:S(2)}, u32[]{:S(2)}) collective-permute-start(s32[128,128]{1,0:T(8,128)S(1)} %pad.23.int_a), channel_id=1, source_target_pairs={{0,1},{1,0},{2,3},{3,2},{4,5},{5,4},{6,7},{7,6},{8,9},{9,8},{10,11... | collective-permute-start | bytes 196616 | tf_op jit(solution)/shard_map/ppermute | solution.py:612
  4.8 15.1 %collective-permute-start.4 = (s32[128,128]{1,0:T(8,128)S(1)}, s32[128,128]{1,0:T(8,128)S(1)}, u32[]{:S(2)}, u32[]{:S(2)}) collective-permute-start(s32[128,128]{1,0:T(8,128)S(1)} %pad.23.int_a), channel_id=1, source_target_pairs={{0,2},{2,0},{1,3},{3,1},{4,6},{6,4},{5,7},{7,5},{8,10},{10,8},{9,1... | collective-permute-start | bytes 196616 | tf_op jit(solution)/shard_map/ppermute | solution.py:611
  5.1 57.4 %collective-permute-start.9 = (bf16[128,768]{1,0:T(8,128)(2,1)}, bf16[128,768]{1,0:T(8,128)(2,1)S(1)}, u32[]{:S(2)}, u32[]{:S(2)}) collective-permute-start(bf16[128,768]{1,0:T(8,128)(2,1)} %cot_a.1), channel_id=1, source_target_pairs={{0,1},{1,0},{2,3},{3,2},{4,5},{5,4},{6,7},{7,6},{8,9},{9,8},{10,11... | collective-permute-start | bytes 589832 | tf_op jit(solution)/shard_map/ppermute | solution.py:612
  20.1 24.9 %collective-permute-start.10 = (bf16[128,768]{1,0:T(8,128)(2,1)S(1)}, bf16[128,768]{1,0:T(8,128)(2,1)S(1)}, u32[]{:S(2)}, u32[]{:S(2)}) collective-permute-start(bf16[128,768]{1,0:T(8,128)(2,1)S(1)} %copy-done.7), channel_id=1, source_target_pairs={{0,2},{2,0},{1,3},{3,1},{4,6},{6,4},{5,7},{7,5},{8,10},{10,8},{9,1... | collective-permute-start | bytes 589832 | tf_op jit(solution)/shard_map/ppermute | solution.py:611
  43.0 9.1 %collective-permute-start.7 = (bf16[576,192]{1,0:T(8,128)(2,1)S(1)}, bf16[576,192]{1,0:T(8,128)(2,1)S(1)}, u32[]{:S(2)}, u32[]{:S(2)}) collective-permute-start(bf16[576,192]{1,0:T(8,128)(2,1)S(1)} %get-tuple-element.53.att_a), channel_id=1, source_target_pairs={{0,2},{2,0},{1,3},{3,1},{4,6},{6,4},{5,7},{7,5},{8,10},{10,8},{9,1... | collective-permute-start | bytes 663560 | tf_op jit(solution)/shard_map/ppermute | solution.py:611
  45.1 17.5 %collective-permute-start.11 = (bf16[128,768]{1,0:T(8,128)(2,1)S(1)}, bf16[128,768]{1,0:T(8,128)(2,1)S(1)}, u32[]{:S(2)}, u32[]{:S(2)}) collective-permute-start(bf16[128,768]{1,0:T(8,128)(2,1)S(1)} %collective-permute-done.10.cot_c), channel_id=1, source_target_pairs={{0,1},{1,0},{2,3},{3,2},{4,5},{5,4},{6,7},{7,6},{8,9},{9,8},{10,11... | collective-permute-start | bytes 589832 | tf_op jit(solution)/shard_map/ppermute | solution.py:613
  45.1 17.4 %collective-permute-start.6 = (bf16[576,192]{1,0:T(8,128)(2,1)S(1)}, bf16[576,192]{1,0:T(8,128)(2,1)S(1)}, u32[]{:S(2)}, u32[]{:S(2)}) collective-permute-start(bf16[576,192]{1,0:T(8,128)(2,1)S(1)} %get-tuple-element.53.att_a), channel_id=1, source_target_pairs={{0,1},{1,0},{2,3},{3,2},{4,5},{5,4},{6,7},{7,6},{8,9},{9,8},{10,11... | collective-permute-start | bytes 663560 | tf_op jit(solution)/shard_map/ppermute | solution.py:612
  52.0 10.5 %collective-permute-start.8 = (bf16[576,192]{1,0:T(8,128)(2,1)S(1)}, bf16[576,192]{1,0:T(8,128)(2,1)S(1)}, u32[]{:S(2)}, u32[]{:S(2)}) collective-permute-start(bf16[576,192]{1,0:T(8,128)(2,1)S(1)} %collective-permute-done.7.att_c), channel_id=1, source_target_pairs={{0,1},{1,0},{2,3},{3,2},{4,5},{5,4},{6,7},{7,6},{8,9},{9,8},{10,11... | collective-permute-start | bytes 663560 | tf_op jit(solution)/shard_map/ppermute | solution.py:613
  73.8 5.6 %collective-permute-start.12 = (bf16[2,144,768]{2,1,0:T(8,128)(2,1)S(1)}, bf16[2,144,768]{2,1,0:T(8,128)(2,1)S(1)}, u32[]{:S(2)}, u32[]{:S(2)}) collective-permute-start(bf16[2,144,768]{2,1,0:T(8,128)(2,1)S(1)} %dynamic-slice_bitcast_fusion.4), channel_id=1, source_target_pairs={{0,1},{1,0},{2,3},{3,2},{4,5},{5,4},{6,7},{7,6},{8,9},{9,8},{10,11... | collective-permute-start | bytes 1327112 | tf_op jit(solution)/shard_map/ppermute | solution.py:623
  74.4 6.7 %collective-permute-start.17 = (bf16[2,144,768]{2,1,0:T(8,128)(2,1)S(1)}, bf16[2,144,768]{2,1,0:T(8,128)(2,1)S(1)}, u32[]{:S(2)}, u32[]{:S(2)}) collective-permute-start(bf16[2,144,768]{2,1,0:T(8,128)(2,1)S(1)} %dynamic-slice_bitcast_fusion.3), channel_id=1, source_target_pairs={{0,1},{1,0},{2,3},{3,2},{4,5},{5,4},{6,7},{7,6},{8,9},{9,8},{10,11... | collective-permute-start | bytes 1327112 | tf_op jit(solution)/shard_map/ppermute | solution.py:623
  75.9 16.2 %collective-permute-start.48 = (bf16[4,96,768]{2,1,0:T(8,128)(2,1)S(1)}, bf16[4,96,768]{2,1,0:T(8,128)(2,1)S(1)}, u32[]{:S(2)}, u32[]{:S(2)}) collective-permute-start(bf16[4,96,768]{2,1,0:T(8,128)(2,1)S(1)} %dynamic-slice_bitcast_fusion.1), channel_id=1, source_target_pairs={{0,4},{4,0},{8,12},{12,8},{16,20},{20,16},{24,28},{28,24},{1,5},{5... | collective-permute-start | bytes 1769480 | tf_op jit(solution)/shard_map/ppermute | solution.py:649
  78.6 25.5 %collective-permute-start.56 = (bf16[4,96,768]{2,1,0:T(8,128)(2,1)S(1)}, bf16[4,96,768]{2,1,0:T(8,128)(2,1)S(1)}, u32[]{:S(2)}, u32[]{:S(2)}) collective-permute-start(bf16[4,96,768]{2,1,0:T(8,128)(2,1)S(1)} %dynamic-slice_bitcast_fusion), channel_id=1, source_target_pairs={{0,4},{4,0},{8,12},{12,8},{16,20},{20,16},{24,28},{28,24},{1,5},{5... | collective-permute-start | bytes 1769480 | tf_op jit(solution)/shard_map/ppermute | solution.py:649
  79.9 26.8 %collective-permute-start.13 = (bf16[144,768]{1,0:T(8,128)(2,1)S(1)}, bf16[144,768]{1,0:T(8,128)(2,1)S(1)}, u32[]{:S(2)}, u32[]{:S(2)}) collective-permute-start(bf16[144,768]{1,0:T(8,128)(2,1)S(1)} %fusion.15), channel_id=1, source_target_pairs={{0,2},{2,0},{1,3},{3,1},{4,6},{6,4},{5,7},{7,5},{8,10},{10,8},{9,1... | collective-permute-start | bytes 663560 | tf_op jit(solution)/shard_map/ppermute | solution.py:624
  81.2 30.2 %collective-permute-start.18 = (bf16[144,768]{1,0:T(8,128)(2,1)S(1)}, bf16[144,768]{1,0:T(8,128)(2,1)S(1)}, u32[]{:S(2)}, u32[]{:S(2)}) collective-permute-start(bf16[144,768]{1,0:T(8,128)(2,1)S(1)} %fusion.16), channel_id=1, source_target_pairs={{0,2},{2,0},{1,3},{3,1},{4,6},{6,4},{5,7},{7,5},{8,10},{10,8},{9,1... | collective-permute-start | bytes 663560 | tf_op jit(solution)/shard_map/ppermute | solution.py:624
  92.3 22.1 %collective-permute-start.49 = (bf16[2,96,768]{2,1,0:T(8,128)(2,1)S(1)}, bf16[2,96,768]{2,1,0:T(8,128)(2,1)}, u32[]{:S(2)}, u32[]{:S(2)}) collective-permute-start(bf16[2,96,768]{2,1,0:T(8,128)(2,1)S(1)} %dynamic-slice_bitcast_fusion.6), channel_id=1, source_target_pairs={{0,8},{4,12},{8,0},{12,4},{16,24},{20,28},{24,16},{28,20},{1,9},{5... | collective-permute-start | bytes 884744 | tf_op jit(solution)/shard_map/ppermute | solution.py:653
  105.1 13.2 %collective-permute-start.57 = (bf16[2,96,768]{2,1,0:T(8,128)(2,1)}, bf16[2,96,768]{2,1,0:T(8,128)(2,1)}, u32[]{:S(2)}, u32[]{:S(2)}) collective-permute-start(bf16[2,96,768]{2,1,0:T(8,128)(2,1)} %dynamic-slice_bitcast_fusion.5), channel_id=1, source_target_pairs={{0,8},{4,12},{8,0},{12,4},{16,24},{20,28},{24,16},{28,20},{1,9},{5... | collective-permute-start | bytes 884744 | tf_op jit(solution)/shard_map/ppermute | solution.py:653
  111.5 20.7 %collective-permute-start.19 = (bf16[144,768]{1,0:T(8,128)(2,1)S(1)}, bf16[144,768]{1,0:T(8,128)(2,1)S(1)}, u32[]{:S(2)}, u32[]{:S(2)}) collective-permute-start(bf16[144,768]{1,0:T(8,128)(2,1)S(1)} %fusion.6.back_a), channel_id=1, source_target_pairs={{0,1},{1,0},{2,3},{3,2},{4,5},{5,4},{6,7},{7,6},{8,9},{9,8},{10,11... | collective-permute-start | bytes 663560 | tf_op jit(solution)/shard_map/ppermute | solution.py:612
  112.1 7.9 %collective-permute-start.20 = (bf16[144,768]{1,0:T(8,128)(2,1)S(1)}, bf16[144,768]{1,0:T(8,128)(2,1)S(1)}, u32[]{:S(2)}, u32[]{:S(2)}) collective-permute-start(bf16[144,768]{1,0:T(8,128)(2,1)S(1)} %fusion.6.back_a), channel_id=1, source_target_pairs={{0,2},{2,0},{1,3},{3,1},{4,6},{6,4},{5,7},{7,5},{8,10},{10,8},{9,1... | collective-permute-start | bytes 663560 | tf_op jit(solution)/shard_map/ppermute | solution.py:611
  115.6 12.8 %collective-permute-start.50 = (bf16[96,768]{1,0:T(8,128)(2,1)S(1)}, bf16[96,768]{1,0:T(8,128)(2,1)S(1)}, u32[]{:S(2)}, u32[]{:S(2)}) collective-permute-start(bf16[96,768]{1,0:T(8,128)(2,1)S(1)} %dynamic-slice_bitcast_fusion.9), channel_id=1, source_target_pairs={{0,16},{4,20},{8,24},{12,28},{16,0},{20,4},{24,8},{28,12},{1,17},{... | collective-permute-start | bytes 442376 | tf_op jit(solution)/shard_map/ppermute | solution.py:654
  119.3 12.2 %collective-permute-start.58 = (bf16[96,768]{1,0:T(8,128)(2,1)S(1)}, bf16[96,768]{1,0:T(8,128)(2,1)S(1)}, u32[]{:S(2)}, u32[]{:S(2)}) collective-permute-start(bf16[96,768]{1,0:T(8,128)(2,1)S(1)} %dynamic-slice_bitcast_fusion.8), channel_id=1, source_target_pairs={{0,16},{4,20},{8,24},{12,28},{16,0},{20,4},{24,8},{28,12},{1,17},{... | collective-permute-start | bytes 442376 | tf_op jit(solution)/shard_map/ppermute | solution.py:654
  120.0 12.9 %collective-permute-start.21 = (bf16[144,768]{1,0:T(8,128)(2,1)S(1)}, bf16[144,768]{1,0:T(8,128)(2,1)S(1)}, u32[]{:S(2)}, u32[]{:S(2)}) collective-permute-start(bf16[144,768]{1,0:T(8,128)(2,1)S(1)} %collective-permute-done.20.back_c), channel_id=1, source_target_pairs={{0,1},{1,0},{2,3},{3,2},{4,5},{5,4},{6,7},{7,6},{8,9},{9,8},{10,11... | collective-permute-start | bytes 663560 | tf_op jit(solution)/shard_map/ppermute | solution.py:613
  129.1 41.8 %collective-permute-start.51 = (bf16[2,24,768]{2,1,0:T(8,128)(2,1)}, bf16[2,24,768]{2,1,0:T(8,128)(2,1)}, u32[]{:S(2)}, u32[]{:S(2)}) collective-permute-start(bf16[2,24,768]{2,1,0:T(8,128)(2,1)} %dynamic-slice_bitcast_fusion.13), channel_id=1, source_target_pairs={{0,1},{1,0},{2,3},{3,2},{4,5},{5,4},{6,7},{7,6},{8,9},{9,8},{10,11... | collective-permute-start | bytes 221192 | tf_op jit(solution)/shard_map/ppermute | solution.py:634
  132.2 51.3 %collective-permute-start.59 = (bf16[96,768]{1,0:T(8,128)(2,1)}, bf16[96,768]{1,0:T(8,128)(2,1)}, u32[]{:S(2)}, u32[]{:S(2)}) collective-permute-start(bf16[96,768]{1,0:T(8,128)(2,1)} %fusion.11), channel_id=1, source_target_pairs={{0,16},{4,20},{8,24},{12,28},{16,0},{20,4},{24,8},{28,12},{1,17},{... | collective-permute-start | bytes 442376 | tf_op jit(solution)/shard_map/ppermute | solution.py:668
  161.5 99.0 %collective-permute-start.22 = (bf16[576,576]{1,0:T(8,128)(2,1)S(1)}, bf16[576,576]{1,0:T(8,128)(2,1)}, u32[]{:S(2)}, u32[]{:S(2)}) collective-permute-start(bf16[576,576]{1,0:T(8,128)(2,1)S(1)} %get-tuple-element.64.dqkv_a), channel_id=1, source_target_pairs={{0,1},{1,0},{2,3},{3,2},{4,5},{5,4},{6,7},{7,6},{8,9},{9,8},{10,11... | collective-permute-start | bytes 1990664 | tf_op jit(solution)/shard_map/ppermute | solution.py:612
  161.5 74.4 %collective-permute-start.23 = (bf16[576,576]{1,0:T(8,128)(2,1)S(1)}, bf16[576,576]{1,0:T(8,128)(2,1)}, u32[]{:S(2)}, u32[]{:S(2)}) collective-permute-start(bf16[576,576]{1,0:T(8,128)(2,1)S(1)} %get-tuple-element.64.dqkv_a), channel_id=1, source_target_pairs={{0,2},{2,0},{1,3},{3,1},{4,6},{6,4},{5,7},{7,5},{8,10},{10,8},{9,1... | collective-permute-start | bytes 1990664 | tf_op jit(solution)/shard_map/ppermute | solution.py:611
  168.6 45.7 %collective-permute-start.31 = (bf16[4,96,576]{2,1,0:T(8,128)(2,1)}, bf16[4,96,576]{2,1,0:T(8,128)(2,1)}, u32[]{:S(2)}, u32[]{:S(2)}) collective-permute-start(bf16[4,96,576]{2,1,0:T(8,128)(2,1)} %dynamic-slice_bitcast_fusion.2), channel_id=1, source_target_pairs={{0,4},{4,0},{8,12},{12,8},{16,20},{20,16},{24,28},{28,24},{1,5},{5... | collective-permute-start | bytes 1327112 | tf_op jit(solution)/shard_map/ppermute | solution.py:649
  171.9 10.0 %collective-permute-start.52 = (bf16[2,24,768]{2,1,0:T(8,128)(2,1)S(1)}, bf16[2,24,768]{2,1,0:T(8,128)(2,1)S(1)}, u32[]{:S(2)}, u32[]{:S(2)}) collective-permute-start(bf16[2,24,768]{2,1,0:T(8,128)(2,1)S(1)} %fusion.30), channel_id=1, source_target_pairs={{0,2},{2,0},{1,3},{3,1},{4,6},{6,4},{5,7},{7,5},{8,10},{10,8},{9,1... | collective-permute-start | bytes 221192 | tf_op jit(solution)/shard_map/ppermute | solution.py:638
  181.9 6.6 %collective-permute-start.39 = (bf16[4,32,768]{2,1,0:T(8,128)(2,1)S(1)}, bf16[4,32,768]{2,1,0:T(8,128)(2,1)S(1)}, u32[]{:S(2)}, u32[]{:S(2)}) collective-permute-start(bf16[4,32,768]{2,1,0:T(8,128)(2,1)S(1)} %fusion.18), channel_id=1, source_target_pairs={{0,4},{4,0},{8,12},{12,8},{16,20},{20,16},{24,28},{28,24},{1,5},{5... | collective-permute-start | bytes 589832 | tf_op jit(solution)/shard_map/ppermute | solution.py:649
  183.5 9.8 %collective-permute-start.53 = (bf16[96,768]{1,0:T(8,128)(2,1)S(1)}, bf16[96,768]{1,0:T(8,128)(2,1)S(1)}, u32[]{:S(2)}, u32[]{:S(2)}) collective-permute-start(bf16[96,768]{1,0:T(8,128)(2,1)S(1)} %bitcast.368), channel_id=1, source_target_pairs={{0,16},{4,20},{8,24},{12,28},{16,0},{20,4},{24,8},{28,12},{1,17},{... | collective-permute-start | bytes 442376 | tf_op jit(solution)/shard_map/ppermute | solution.py:668
  188.6 18.4 %collective-permute-start.60 = (bf16[2,96,768]{2,1,0:T(8,128)(2,1)S(1)}, bf16[2,96,768]{2,1,0:T(8,128)(2,1)S(1)}, u32[]{:S(2)}, u32[]{:S(2)}) collective-permute-start(bf16[2,96,768]{2,1,0:T(8,128)(2,1)S(1)} %pad_maximum_fusion.8), channel_id=1, source_target_pairs={{0,8},{4,12},{8,0},{12,4},{16,24},{20,28},{24,16},{28,20},{1,9},{5... | collective-permute-start | bytes 884744 | tf_op jit(solution)/shard_map/ppermute | solution.py:669
  193.3 7.4 %collective-permute-start.40 = (bf16[2,32,768]{2,1,0:T(8,128)(2,1)S(1)}, bf16[2,32,768]{2,1,0:T(8,128)(2,1)S(1)}, u32[]{:S(2)}, u32[]{:S(2)}) collective-permute-start(bf16[2,32,768]{2,1,0:T(8,128)(2,1)S(1)} %dynamic-slice_bitcast_fusion.11), channel_id=1, source_target_pairs={{0,8},{4,12},{8,0},{12,4},{16,24},{20,28},{24,16},{28,20},{1,9},{5... | collective-permute-start | bytes 294920 | tf_op jit(solution)/shard_map/ppermute | solution.py:653
  200.8 5.6 %collective-permute-start.41 = (bf16[32,768]{1,0:T(8,128)(2,1)S(1)}, bf16[32,768]{1,0:T(8,128)(2,1)S(1)}, u32[]{:S(2)}, u32[]{:S(2)}) collective-permute-start(bf16[32,768]{1,0:T(8,128)(2,1)S(1)} %dynamic-slice_bitcast_fusion.15), channel_id=1, source_target_pairs={{0,16},{4,20},{8,24},{12,28},{16,0},{20,4},{24,8},{28,12},{1,17},{... | collective-permute-start | bytes 147464 | tf_op jit(solution)/shard_map/ppermute | solution.py:654
  206.4 17.2 %collective-permute-start.54 = (bf16[2,96,768]{2,1,0:T(8,128)(2,1)S(1)}, bf16[2,96,768]{2,1,0:T(8,128)(2,1)S(1)}, u32[]{:S(2)}, u32[]{:S(2)}) collective-permute-start(bf16[2,96,768]{2,1,0:T(8,128)(2,1)S(1)} %pad_maximum_fusion.7), channel_id=1, source_target_pairs={{0,8},{4,12},{8,0},{12,4},{16,24},{20,28},{24,16},{28,20},{1,9},{5... | collective-permute-start | bytes 884744 | tf_op jit(solution)/shard_map/ppermute | solution.py:669
  212.2 36.9 %collective-permute-start.61 = (bf16[2,2,96,768]{3,2,1,0:T(8,128)(2,1)}, bf16[2,2,96,768]{3,2,1,0:T(8,128)(2,1)}, u32[]{:S(2)}, u32[]{:S(2)}) collective-permute-start(bf16[2,2,96,768]{3,2,1,0:T(8,128)(2,1)} %pad_maximum_fusion.3), channel_id=1, source_target_pairs={{0,4},{4,0},{8,12},{12,8},{16,20},{20,16},{24,28},{28,24},{1,5},{5... | collective-permute-start | bytes 1769480 | tf_op jit(solution)/shard_map/ppermute | solution.py:670
  214.3 7.2 %collective-permute-start.43 = (bf16[2,32,768]{2,1,0:T(8,128)(2,1)S(1)}, bf16[2,32,768]{2,1,0:T(8,128)(2,1)S(1)}, u32[]{:S(2)}, u32[]{:S(2)}) collective-permute-start(bf16[2,32,768]{2,1,0:T(8,128)(2,1)S(1)} %pad_maximum_fusion.16), channel_id=1, source_target_pairs={{0,8},{4,12},{8,0},{12,4},{16,24},{20,28},{24,16},{28,20},{1,9},{5... | collective-permute-start | bytes 294920 | tf_op jit(solution)/shard_map/ppermute | solution.py:669
  221.4 6.6 %collective-permute-start.32 = (bf16[2,96,576]{2,1,0:T(8,128)(2,1)S(1)}, bf16[2,96,576]{2,1,0:T(8,128)(2,1)S(1)}, u32[]{:S(2)}, u32[]{:S(2)}) collective-permute-start(bf16[2,96,576]{2,1,0:T(8,128)(2,1)S(1)} %dynamic-slice_bitcast_fusion.7), channel_id=1, source_target_pairs={{0,8},{4,12},{8,0},{12,4},{16,24},{20,28},{24,16},{28,20},{1,9},{5... | collective-permute-start | bytes 663560 | tf_op jit(solution)/shard_map/ppermute | solution.py:653
  223.5 6.5 %collective-permute-start.44 = (bf16[2,2,32,768]{3,2,0,1:T(8,128)(2,1)S(1)}, bf16[2,2,32,768]{3,2,0,1:T(8,128)(2,1)S(1)}, u32[]{:S(2)}, u32[]{:S(2)}) collective-permute-start(bf16[2,2,32,768]{3,2,0,1:T(8,128)(2,1)S(1)} %pad_maximum_fusion.11), channel_id=1, source_target_pairs={{0,4},{4,0},{8,12},{12,8},{16,20},{20,16},{24,28},{28,24},{1,5},{5... | collective-permute-start | bytes 589832 | tf_op jit(solution)/shard_map/ppermute | solution.py:670
  228.8 6.1 %collective-permute-start.33 = (bf16[96,576]{1,0:T(8,128)(2,1)}, bf16[96,576]{1,0:T(8,128)(2,1)}, u32[]{:S(2)}, u32[]{:S(2)}) collective-permute-start(bf16[96,576]{1,0:T(8,128)(2,1)} %dynamic-slice_bitcast_fusion.10), channel_id=1, source_target_pairs={{0,16},{4,20},{8,24},{12,28},{16,0},{20,4},{24,8},{28,12},{1,17},{... | collective-permute-start | bytes 331784 | tf_op jit(solution)/shard_map/ppermute | solution.py:654
  235.9 22.3 %collective-permute-start.55 = (bf16[2,2,96,768]{3,2,1,0:T(8,128)(2,1)}, bf16[2,2,96,768]{3,2,1,0:T(8,128)(2,1)}, u32[]{:S(2)}, u32[]{:S(2)}) collective-permute-start(bf16[2,2,96,768]{3,2,1,0:T(8,128)(2,1)} %pad_maximum_fusion.2), channel_id=1, source_target_pairs={{0,4},{4,0},{8,12},{12,8},{16,20},{20,16},{24,28},{28,24},{1,5},{5... | collective-permute-start | bytes 1769480 | tf_op jit(solution)/shard_map/ppermute | solution.py:670
  236.8 23.6 %collective-permute-start.24 = (bf16[576,576]{1,0:T(8,128)(2,1)}, bf16[576,576]{1,0:T(8,128)(2,1)S(1)}, u32[]{:S(2)}, u32[]{:S(2)}) collective-permute-start(bf16[576,576]{1,0:T(8,128)(2,1)} %collective-permute-done.23.dqkv_c), channel_id=1, source_target_pairs={{0,1},{1,0},{2,3},{3,2},{4,5},{5,4},{6,7},{7,6},{8,9},{9,8},{10,11... | collective-permute-start | bytes 1990664 | tf_op jit(solution)/shard_map/ppermute | solution.py:613
  246.1 5.9 %collective-permute-start.36 = (bf16[96,576]{1,0:T(8,128)(2,1)S(1)}, bf16[96,576]{1,0:T(8,128)(2,1)S(1)}, u32[]{:S(2)}, u32[]{:S(2)}) collective-permute-start(bf16[96,576]{1,0:T(8,128)(2,1)S(1)} %bitcast.371), channel_id=1, source_target_pairs={{0,16},{4,20},{8,24},{12,28},{16,0},{20,4},{24,8},{28,12},{1,17},{... | collective-permute-start | bytes 331784 | tf_op jit(solution)/shard_map/ppermute | solution.py:668
  252.7 22.1 %collective-permute-start.37 = (bf16[2,96,576]{2,1,0:T(8,128)(2,1)}, bf16[2,96,576]{2,1,0:T(8,128)(2,1)}, u32[]{:S(2)}, u32[]{:S(2)}) collective-permute-start(bf16[2,96,576]{2,1,0:T(8,128)(2,1)} %pad_maximum_fusion.9), channel_id=1, source_target_pairs={{0,8},{4,12},{8,0},{12,4},{16,24},{20,28},{24,16},{28,20},{1,9},{5... | collective-permute-start | bytes 663560 | tf_op jit(solution)/shard_map/ppermute | solution.py:669
  274.2 7.9 %collective-permute-start.25 = (bf16[4,32,768]{2,1,0:T(8,128)(2,1)S(1)}, bf16[4,32,768]{2,1,0:T(8,128)(2,1)S(1)}, u32[]{:S(2)}, u32[]{:S(2)}) collective-permute-start(bf16[4,32,768]{2,1,0:T(8,128)(2,1)S(1)} %fusion.22), channel_id=1, source_target_pairs={{0,4},{4,0},{8,12},{12,8},{16,20},{20,16},{24,28},{28,24},{1,5},{5... | collective-permute-start | bytes 589832 | tf_op jit(solution)/shard_map/ppermute | solution.py:649
  275.9 13.6 %collective-permute-start.38 = (bf16[2,2,96,576]{3,2,1,0:T(8,128)(2,1)S(1)}, bf16[2,2,96,576]{3,2,1,0:T(8,128)(2,1)S(1)}, u32[]{:S(2)}, u32[]{:S(2)}) collective-permute-start(bf16[2,2,96,576]{3,2,1,0:T(8,128)(2,1)S(1)} %pad_maximum_fusion.4), channel_id=1, source_target_pairs={{0,4},{4,0},{8,12},{12,8},{16,20},{20,16},{24,28},{28,24},{1,5},{5... | collective-permute-start | bytes 1327112 | tf_op jit(solution)/shard_map/ppermute | solution.py:670
  287.0 6.5 %collective-permute-start.27 = (bf16[32,768]{1,0:T(8,128)(2,1)S(1)}, bf16[32,768]{1,0:T(8,128)(2,1)S(1)}, u32[]{:S(2)}, u32[]{:S(2)}) collective-permute-start(bf16[32,768]{1,0:T(8,128)(2,1)S(1)} %dynamic-slice_bitcast_fusion.16), channel_id=1, source_target_pairs={{0,16},{4,20},{8,24},{12,28},{16,0},{20,4},{24,8},{28,12},{1,17},{... | collective-permute-start | bytes 147464 | tf_op jit(solution)/shard_map/ppermute | solution.py:654
  303.5 8.5 %collective-permute-start.30 = (bf16[2,2,32,768]{3,2,0,1:T(8,128)(2,1)S(1)}, bf16[2,2,32,768]{3,2,0,1:T(8,128)(2,1)}, u32[]{:S(2)}, u32[]{:S(2)}) collective-permute-start(bf16[2,2,32,768]{3,2,0,1:T(8,128)(2,1)S(1)} %pad_maximum_fusion.10), channel_id=1, source_target_pairs={{0,4},{4,0},{8,12},{12,8},{16,20},{20,16},{24,28},{28,24},{1,5},{5... | collective-permute-start | bytes 589832 | tf_op jit(solution)/shard_map/ppermute | solution.py:670
  (60 other events, 333.2 us)
